TPU v7x, 128 devices: a whole 4x4x4 slice. The times are simulated.
128 devices in a mesh: freq: 4 (over z), space: 32 (over x, y, core).
Axes of the slice: x: 4, y: 4, z: 4, core: 2. Of those that a mesh axis runs over, the one named last changes fastest.
Arguments:
- recorded: bfloat16 [8, 2, 8192, 128], P('freq', None, 'space'), may hold values from -6 to 6
- v_factors: bfloat16 [8, 32, 2, 8192, 128], P('freq', None, None, 'space'), may hold values from -0.25 to 0.25
- u_factors: bfloat16 [8, 2, 8192, 32, 128], P('freq', None, 'space'), may hold values from -0.125 to 0.125
- tile_ranks: int32 [8, 32, 32], P('freq'), may hold values from 0 to 128, as said below
- mute_start: int32 [8192, 128], P('space', 'freq'), may hold values from 0 to 127
Outputs:
- muted_traces: float32 [8192, 128, 128], P('space', 'freq')
Inputs may be any that keep to these rules, and one draw needn't show every extreme that they name: `tile_ranks`: entries with i equal to j are 128; every other entry is 0 or 64.
All inputs are finite; a program needn't handle non-finite values.
Results may differ from a plain program's by a relative error of at most 0.0041.
Values may be sent and summed in bfloat16 or wider, within the bound.
No kernel may reach another device: no remote copies, remote signals or barrier semaphores. Data moves between devices by JAX's collectives and lax.ppermute only.
A program may use at most 64 MiB of HBM per device.

v0:
```python
import math

import jax
import jax.numpy as jnp
from jax import lax
from jax.sharding import PartitionSpec as P

NT = 128


def apply_rows(received, row_factors):
    freq_count = received.shape[0]
    merged = received.reshape(
        freq_count, received.shape[1] * received.shape[2], 2, received.shape[4]
    )
    products = jnp.einsum(
        "fcpm,fmbs->fcpbs", row_factors, merged, preferred_element_type=jnp.float32
    )
    real_part = products[:, 0, :, 0] - products[:, 1, :, 1]
    imag_part = products[:, 0, :, 1] + products[:, 1, :, 0]
    return jnp.stack([real_part, imag_part], axis=1)


def time_basis(count, freq_total):
    freq_index = lax.iota(jnp.int32, count)
    weights = 1 + freq_index * (NT // 2 // freq_total)
    times = lax.iota(jnp.int32, NT)
    phase = (weights[:, None] * times[None, :] % NT).astype(jnp.float32) * (2.0 * math.pi / NT)
    scale = 1.0 / math.sqrt(2.0 * freq_total)
    return (jnp.cos(phase) * scale, -jnp.sin(phase) * scale)


def to_time(spectra, cos_basis, sin_basis):
    spectra_float = spectra.astype(jnp.float32)
    high = lax.Precision.HIGHEST
    return jnp.einsum("fps,ft->pst", spectra_float[:, 0], cos_basis, precision=high) + jnp.einsum(
        "fps,ft->pst", spectra_float[:, 1], sin_basis, precision=high
    )


def gathered_time(spectra, freq_total):
    cos_basis, sin_basis = time_basis(freq_total, freq_total)
    return to_time(spectra, cos_basis, sin_basis)


def shards(recorded, v_factors, u_factors, tile_ranks, mute_start):
    freq_count = recorded.shape[0]
    tile_rows = recorded.shape[2]
    tile_count = lax.axis_size("space")
    rank_width = v_factors.shape[4]
    half_width = rank_width // 2
    freq_total = freq_count * lax.axis_size("freq")
    column = lax.axis_index("space")
    real_in = recorded[:, 0]
    imag_in = recorded[:, 1]
    upper_half = jnp.stack([real_in, imag_in], axis=2)
    lower_half = jnp.stack([-imag_in, real_in], axis=2)
    stacked = jnp.concatenate([upper_half, lower_half], axis=1)
    column_factors = v_factors.reshape(freq_count, tile_count, 2 * tile_rows, rank_width)
    column_ranks = lax.dynamic_index_in_dim(tile_ranks, column, 2, keepdims=False)
    rank_index = lax.iota(jnp.int32, rank_width)
    low_factors = column_factors[:, :, :, :half_width]
    send_blocks = jnp.einsum(
        "fiak,fabs->fikbs", low_factors, stacked, preferred_element_type=jnp.float32
    )
    kept = rank_index[None, None, :half_width] < column_ranks[:, :, None]
    send_blocks = jnp.where(kept[:, :, :, None, None], send_blocks, 0.0).astype(jnp.bfloat16)
    send_factors = u_factors[:, :, :, :, :half_width].reshape(
        freq_count, 2, tile_rows, tile_count * half_width
    )
    own_v = lax.dynamic_index_in_dim(v_factors, column, 1, keepdims=False)[:, :, :, half_width:]
    own_v = own_v.reshape(freq_count, 2 * tile_rows, rank_width - half_width)
    own_blocks = jnp.einsum("fak,fabs->fkbs", own_v, stacked, preferred_element_type=jnp.float32)
    own_rank = lax.dynamic_index_in_dim(column_ranks, column, 1, keepdims=False)
    own_kept = rank_index[None, half_width:] < own_rank[:, None]
    own_blocks = jnp.where(own_kept[:, :, None, None], own_blocks, 0.0).astype(jnp.bfloat16)
    own_u = lax.dynamic_index_in_dim(u_factors, column, 3, keepdims=False)[:, :, :, half_width:]
    extra = apply_rows(own_blocks[:, None], own_u)
    summed = apply_rows(
        lax.all_to_all(send_blocks, "space", split_axis=1, concat_axis=1, tiled=True),
        row_factors=send_factors,
    )
    spectra = (summed + extra).astype(jnp.bfloat16)
    traces = gathered_time(
        lax.all_to_all(spectra, "freq", split_axis=3, concat_axis=0, tiled=True),
        freq_total=freq_total,
    )
    times = lax.iota(jnp.int32, NT)
    return jnp.where(times[None, None, :] >= mute_start[:, :, None], traces, 0.0)


def solution(mesh):
    placed = (
        P("freq", None, "space", None),
        P("freq", None, None, "space", None),
        P("freq", None, "space", None, None),
        P("freq", None, None),
        P("space", "freq"),
    )
    return jax.shard_map(
        shards, mesh=mesh, in_specs=placed, out_specs=P("space", "freq", None), check_vma=False
    )
```

profile of v0, /device:TPU:0, one launch (start us, length us, event | category | flops | bytes accessed | tf_op | source)
XLA Modules:
  0.0 72.3 jit_solution(1147717936734768422)
XLA Ops:
  0.0 1.0 %slice_bitcast_fusion.11 = (bf16[2,256,1,128]{3,1,2,0:T(8,128)(2,1)S(1)}, bf16[2,256,1,128]{3,1,2,0:T(8,128)(2,1)S(1)}) fusion(bf16[2,2,256,128]{3,2,1,0:T(8,128)(2,1)} %param.5), kind=kLoop, calls=%fused_computation.32 | loop fusion | bytes 524288 | tf_op jit(solution)/shard_map/stack;squeeze | solution.py:56
  1.0 1.0 %fusion.44 = bf16[2,256,1,128]{3,1,2,0:T(8,128)(2,1)S(1)} fusion(bf16[2,2,256,128]{3,2,1,0:T(8,128)(2,1)} %param.5), kind=kLoop, calls=%fused_computation.71 | loop fusion | flops 65536 | bytes 262144 | tf_op jit(solution)/shard_map/neg | solution.py:57
  2.0 0.2 dynamic-slice_reduce_fusion
  2.3 5.3 %fusion.1 = bf16[2,32,64,2,128]{4,2,1,3,0:T(8,128)(2,1)S(1)} fusion(pred[2,32,64]{2,1,0:T(8,128)(4,1)S(1)} %broadcast_compare_fusion, bf16[2,32,512,128]{3,2,1,0:T(8,128)(2,1)} %bitcast.102, bf16[2,256,1,128]{3,1,2,0:T(8,128)(2,1)S(1)} %get-tuple-element.8, bf16[2,256,1,128]{3,1,2,0:T(8,128)(2,1)S(1)} %fusion.44, ...), kind=kOutput, calls=%fused_computation.5 | convolution fusion | flops 1077936128 | bytes 10883072 | tf_op jit(solution)/shard_map/fiak,fabs->fikbs/dot_general | solution.py:63
  7.6 1.5 %copy.54 = bf16[2,32,64,2,128]{4,2,3,0,1:T(8,128)(2,1)} copy(bf16[2,32,64,2,128]{4,2,1,3,0:T(8,128)(2,1)S(1)} %fusion.1) | data formatting | bytes 4194304 | tf_op jit(solution)/shard_map/convert_element_type | solution.py:67
  9.1 7.4 %all-to-all-start = ((bf16[2,32,64,2,128]{4,2,3,0,1:T(8,128)(2,1)}), bf16[2,32,64,2,128]{4,2,3,0,1:T(8,128)(2,1)S(1)}, u32[]{:S(2)}, u32[]{:S(2)}) async-start(bf16[2,32,64,2,128]{4,2,3,0,1:T(8,128)(2,1)} %copy.54), calls=%async_computation | async-start | bytes 4194304 | tf_op jit(solution)/shard_map/all_to_all | solution.py:80
  16.6 1.0 %dynamic-slice_bitcast_fusion = bf16[2,2,256,128]{3,2,1,0:T(8,128)(2,1)S(1)} fusion(bf16[2,32,2,256,128]{4,3,2,1,0:T(8,128)(2,1)} %param.6, s32[]{:T(128)S(6)} %select_n.34), kind=kLoop, calls=%fused_computation.25 | loop fusion | bytes 524292 | tf_op jit(solution)/shard_map/jit(dynamic_index_in_dim)/squeeze | solution.py:71
  17.8 2.1 %constant_dynamic-slice_fusion = bf16[2,2,256,1,128]{4,3,2,1,0:T(2,128)(2,1)S(1)} fusion(bf16[2,2,256,32,128]{4,3,2,1,0:T(8,128)(2,1)} %param.7, s32[]{:T(128)S(6)} %select_n.34), kind=kLoop, calls=%fused_computation.58 | loop fusion | bytes 524292 | tf_op jit(solution)/shard_map/jit(dynamic_index_in_dim)/dynamic_slice | solution.py:77
  19.9 0.4 copy.61
  20.3 10.4 %copy.90 = bf16[2,2,256,32,64]{2,4,3,1,0:T(8,128)(2,1)} copy(bf16[2,2,256,32,64]{4,3,2,1,0:T(8,128)(2,1)} %bitcast.95) | data formatting | bytes 8388608
  30.7 0.2 dynamic-slice_reduce_fusion.1
  30.9 0.3 fusion.3
  31.2 0.3 fusion.12
  31.5 13.9 %all-to-all-done = bf16[2,32,64,2,128]{4,2,3,0,1:T(8,128)(2,1)S(1)} async-done(((bf16[2,32,64,2,128]{4,2,3,0,1:T(8,128)(2,1)}), bf16[2,32,64,2,128]{4,2,3,0,1:T(8,128)(2,1)S(1)}, u32[]{:S(2)}, u32[]{:S(2)}) %all-to-all-start) | async-done | bytes 2097184 | tf_op jit(solution)/shard_map/all_to_all | solution.py:80
  45.5 0.2 copy.55
  45.7 2.0 %copy-done.1 = bf16[2,2,256,32,64]{2,4,3,1,0:T(8,128)(2,1)S(1)} copy-done((bf16[2,2,256,32,64]{2,4,3,1,0:T(8,128)(2,1)S(1)}, bf16[2,2,256,32,64]{2,4,3,1,0:T(8,128)(2,1)}, u32[]{:S(2)}) %copy-start.1) | copy-done | bytes 4194328
  47.7 1.3 %convolution_bitcast_fusion = f32[2,2,256,2,128]{2,4,1,3,0:T(8,128)S(1)} fusion(bf16[2,2048,2,128,1]{3,1,4,2,0:T(8,128)(2,1)S(1)} %bitcast.97, bf16[2,2,256,2048,1]{2,3,1,4,0:T(8,128)(2,1)S(1)} %bitcast.96), kind=kOutput, calls=%fused_computation.6 | convolution fusion | flops 1073741824 | bytes 7340032 | tf_op jit(solution)/shard_map/fcpm,fmbs->fcpbs/dot_general | solution.py:16
  49.2 1.0 %copy.68 = bf16[2,2,256,128]{2,0,1,3:T(2,128)(2,1)} copy(bf16[2,2,256,128]{2,3,0,1:T(8,128)(2,1)S(1)} %fusion.4) | data formatting | bytes 524288 | tf_op jit(solution)/shard_map/convert_element_type | solution.py:83
  50.2 5.3 %all-to-all-start.1 = ((bf16[2,2,256,128]{2,0,1,3:T(2,128)(2,1)}), bf16[2,2,256,128]{2,0,1,3:T(2,128)(2,1)S(1)}, u32[]{:S(2)}, u32[]{:S(2)}) async-start(bf16[2,2,256,128]{2,0,1,3:T(2,128)(2,1)} %copy.68), calls=%async_computation.1 | async-start | bytes 524288 | tf_op jit(solution)/shard_map/all_to_all | solution.py:85
  55.5 6.7 %all-to-all-done.1 = bf16[2,2,256,128]{2,0,1,3:T(2,128)(2,1)S(1)} async-done(((bf16[2,2,256,128]{2,0,1,3:T(2,128)(2,1)}), bf16[2,2,256,128]{2,0,1,3:T(2,128)(2,1)S(1)}, u32[]{:S(2)}, u32[]{:S(2)}) %all-to-all-start.1) | async-done | bytes 262176 | tf_op jit(solution)/shard_map/all_to_all | solution.py:85
  62.2 0.2 copy.99
  62.5 2.4 %fusion.11 = f32[256,32,128]{2,0,1:T(8,128)S(1)} fusion(bf16[8,2,256,32]{2,0,3,1:T(8,128)(2,1)S(1)} %all_to_all.20, s32[8]{0:T(128)S(1)} %multiply_add_fusion), kind=kOutput, calls=%fused_computation.28 | convolution fusion | flops 100678656 | bytes 4325888 | tf_op jit(solution)/shard_map/fps,ft->pst/dot_general | solution.py:36
  64.8 3.0 %add_select_fusion = f32[256,32,128]{2,0,1:T(8,128)S(1)} fusion(f32[256,32,128]{2,0,1:T(8,128)S(1)} %fusion.11, s32[256,32]{0,1:T(8,128)S(1)} %copy-done.4, bf16[8,2,256,32]{2,0,3,1:T(8,128)(2,1)S(1)} %all_to_all.20, s32[8]{0:T(128)S(1)} %multiply_add_fusion), kind=kOutput, calls=%fused_computation.2 | convolution fusion | flops 103825408 | bytes 8552960 | tf_op jit(solution)/shard_map/fps,ft->pst/dot_general | solution.py:36
  67.8 4.4 %copy.70 = f32[256,32,128]{2,1,0:T(8,128)} copy(f32[256,32,128]{2,0,1:T(8,128)S(1)} %add_select_fusion) | data formatting | bytes 8388608 | tf_op jit(solution)/shard_map/jit(_where)/select_n | solution.py:89
  (20 shorter events, 0.7 us)
Async XLA Ops:
  0.0 2.0 %copy-start = (s32[2,32,32]{2,1,0:T(8,128)S(1)}, s32[2,32,32]{2,1,0:T(8,128)}, u32[]{:S(2)}) copy-start(s32[2,32,32]{2,1,0:T(8,128)} %param.8) | copy-start | bytes 24580
  1.0 6.6 %copy-start.2 = (bf16[2,256,1,128]{3,1,2,0:T(8,128)(2,1)}, bf16[2,256,1,128]{3,1,2,0:T(8,128)(2,1)S(1)}, u32[]{:S(2)}) copy-start(bf16[2,256,1,128]{3,1,2,0:T(8,128)(2,1)S(1)} %get-tuple-element.8) | copy-start | bytes 393220
  9.1 36.3 %all-to-all-start = ((bf16[2,32,64,2,128]{4,2,3,0,1:T(8,128)(2,1)}), bf16[2,32,64,2,128]{4,2,3,0,1:T(8,128)(2,1)S(1)}, u32[]{:S(2)}, u32[]{:S(2)}) async-start(bf16[2,32,64,2,128]{4,2,3,0,1:T(8,128)(2,1)} %copy.54), calls=%async_computation | async-start | bytes 4194304 | tf_op jit(solution)/shard_map/all_to_all | solution.py:80
  20.3 10.7 %copy-start.3 = (bf16[2,256,1,128]{3,1,2,0:T(8,128)(2,1)S(1)}, bf16[2,256,1,128]{3,1,2,0:T(8,128)(2,1)}, u32[]{:S(2)}) copy-start(bf16[2,256,1,128]{3,1,2,0:T(8,128)(2,1)} %copy-done.2) | copy-start | bytes 393220
  45.5 2.2 %copy-start.1 = (bf16[2,2,256,32,64]{2,4,3,1,0:T(8,128)(2,1)S(1)}, bf16[2,2,256,32,64]{2,4,3,1,0:T(8,128)(2,1)}, u32[]{:S(2)}) copy-start(bf16[2,2,256,32,64]{2,4,3,1,0:T(8,128)(2,1)} %copy.90) | copy-start | bytes 12582916
  49.1 15.7 %copy-start.4 = (s32[256,32]{0,1:T(8,128)S(1)}, s32[256,32]{0,1:T(8,128)}, u32[]{:S(2)}) copy-start(s32[256,32]{0,1:T(8,128)} %param.9) | copy-start | bytes 98308
  50.2 12.0 %all-to-all-start.1 = ((bf16[2,2,256,128]{2,0,1,3:T(2,128)(2,1)}), bf16[2,2,256,128]{2,0,1,3:T(2,128)(2,1)S(1)}, u32[]{:S(2)}, u32[]{:S(2)}) async-start(bf16[2,2,256,128]{2,0,1,3:T(2,128)(2,1)} %copy.68), calls=%async_computation.1 | async-start | bytes 524288 | tf_op jit(solution)/shard_map/all_to_all | solution.py:85
where the time goes:
time: 72.9 us; the launch traced here: 72.3 us
  local copies, waits for them, and re-layouts  24.8 us (34%)
  waiting for transfers between devices  20.6 us (28%)
  starting transfers between devices  12.7 us (17%)
  matrix products  12.5 us (17%)
  other arithmetic  1.35 us (2%)
    all_to_all x1, waiting for transfers between devices, shards(): lax.all_to_all(send_blocks, 'space', split_axis=1, concat_axis=1, tiled=T...  13.9 us
    unnamed x11, local copies, waits for them, and re-layouts  12.4 us
    all_to_all x1, starting transfers between devices, shards(): lax.all_to_all(send_blocks, 'space', split_axis=1, concat_axis=1, tiled=T...  7.4 us
    all_to_all x1, waiting for transfers between devices, shards(): lax.all_to_all(spectra, 'freq', split_axis=3, concat_axis=0, tiled=True)  6.67 us
    dot_general x1, matrix products, shards(): jnp.einsum('fiak,fabs->fikbs', low_factors, stacked, preferred_element_ty...  5.33 us
    all_to_all x1, starting transfers between devices, shards(): lax.all_to_all(spectra, 'freq', split_axis=3, concat_axis=0, tiled=True)  5.31 us
    select_n x1, local copies, waits for them, and re-layouts, shards(): jnp.where(times[None, None, :] >= mute_start[:, :, None], traces, 0.0)  4.44 us
    dot_general x1, matrix products, to_time(): jnp.einsum('fps,ft->pst', spectra_float[:, 1], sin_basis, precision=high)  2.96 us
  transfers between devices with their start and end apart: 2, of which 2 were waited for; matrix products, arithmetic and copies ran while one was open for 21% of the time, Pallas kernels for 0%

commit v1 on v0

v1 whole, which is shorter than its diff:
```python
import math

import jax
import jax.numpy as jnp
import numpy as np
from jax import lax
from jax.experimental import pallas as pl
from jax.experimental.pallas import tpu as pltpu
from jax.sharding import PartitionSpec as P

NT = 128
MIB = 1024 * 1024


def params(vmem):
    return pltpu.CompilerParams(vmem_limit_bytes=vmem * MIB)


def lane_index(shape):
    return lax.broadcasted_iota(jnp.int32, shape, len(shape) - 1)


def row_index(shape):
    return lax.broadcasted_iota(jnp.int32, shape, len(shape) - 2)


def stack_sources(recorded_ref, stacked_ref):
    for f in range(2):
        real = recorded_ref[f, 0]
        imag = recorded_ref[f, 1]
        stacked_ref[f, 0:256, 0:128] = real
        stacked_ref[f, 256:512, 0:128] = -imag
        stacked_ref[f, 0:256, 128:256] = imag
        stacked_ref[f, 256:512, 128:256] = real


def transposed_dot(factors, stacked):
    return lax.dot_general(
        factors.reshape(512, 128),
        stacked,
        (((0,), (0,)), ((), ())),
        preferred_element_type=jnp.float32,
    )


def blocks_kernel(
    ranks_hbm, recorded_hbm, v_hbm, send_hbm,
    ranks, recorded, stacked, factors, blocks, small_sem, v_sem, send_sem,
):
    column = lax.axis_index("space")
    tile_count = factors.shape[1]
    parts = send_sem.shape[0]
    width = tile_count // parts
    get_ranks = pltpu.make_async_copy(ranks_hbm, ranks, small_sem.at[0])
    get_recorded = pltpu.make_async_copy(recorded_hbm, recorded, small_sem.at[1])
    get_ranks.start()
    get_recorded.start()

    def get_tile(f, i):
        return pltpu.make_async_copy(v_hbm.at[f, i], factors.at[f, i], v_sem.at[f, i])

    def get_first(f):
        first = pl.ds(0, width)
        return pltpu.make_async_copy(v_hbm.at[f, first], factors.at[f, first], v_sem.at[f, 0])

    def put_part(part):
        rows = pl.ds(part * width, width)
        return pltpu.make_async_copy(blocks.at[rows], send_hbm.at[rows], send_sem.at[part])

    for f in range(2):
        get_first(f).start()
    get_ranks.wait()

    @pl.loop(width, tile_count)
    def _(i):
        for f in range(2):

            @pl.when(ranks[tile_count * f + i, column] > 0)
            def _():
                get_tile(f, i).start()

    get_recorded.wait()
    stack_sources(recorded, stacked)
    row = row_index((64, 256))
    for part in range(parts):
        if part == 0:
            for f in range(2):
                get_first(f).wait()
        else:
            for i in range(part * width, (part + 1) * width):
                for f in range(2):

                    @pl.when(ranks[tile_count * f + i, column] > 0)
                    def _():
                        get_tile(f, i).wait()

        for i in range(part * width, (part + 1) * width):
            for f in range(2):
                product = transposed_dot(factors[f, i], stacked[f])[0:64]
                kept = row < ranks[tile_count * f + i, column]
                blocks[i, f * 64 : (f + 1) * 64] = jnp.where(kept, product, 0.0).astype(
                    jnp.bfloat16
                )
        put_part(part).start()
    for part in range(parts):
        put_part(part).wait()


def make_blocks(recorded, v_factors, ranks, parts=4):
    tile_count = v_factors.shape[1]
    return pl.pallas_call(
        blocks_kernel,
        in_specs=[pl.BlockSpec(memory_space=pl.ANY)] * 3,
        out_specs=pl.BlockSpec(memory_space=pltpu.HBM),
        out_shape=jax.ShapeDtypeStruct((tile_count, 128, 256), jnp.bfloat16),
        scratch_shapes=[
            pltpu.SMEM(ranks.shape, jnp.int32),
            pltpu.VMEM((2, 2, 256, 128), jnp.bfloat16),
            pltpu.VMEM((2, 512, 256), jnp.bfloat16),
            pltpu.VMEM((2, tile_count, 2, 256, 128), jnp.bfloat16),
            pltpu.VMEM((tile_count, 128, 256), jnp.bfloat16),
            pltpu.SemaphoreType.DMA((2,)),
            pltpu.SemaphoreType.DMA((2, tile_count)),
            pltpu.SemaphoreType.DMA((parts,)),
        ],
        compiler_params=params(60),
        cost_estimate=pl.CostEstimate(
            flops=4 * 10**9, bytes_accessed=11 * 10**6, transcendentals=0
        ),
        name="blocks",
    )(ranks, recorded, v_factors)


def own_kernel(ranks_hbm, recorded_ref, v_hbm, high_ref, ranks, factors, stacked, sem):
    column = lax.axis_index("space")
    get_ranks = pltpu.make_async_copy(ranks_hbm, ranks, sem.at[0])
    get_ranks.start()
    copies = [
        pltpu.make_async_copy(v_hbm.at[f, column], factors.at[f], sem.at[1 + f]) for f in range(2)
    ]
    for copy in copies:
        copy.start()
    stack_sources(recorded_ref, stacked)
    get_ranks.wait()
    row = row_index((64, 256)) + 64
    for f in range(2):
        copies[f].wait()
        product = transposed_dot(factors[f], stacked[f])[64:128]
        kept = row < ranks[ranks.shape[1] * f + column, column]
        high_ref[f * 64 : (f + 1) * 64] = jnp.where(kept, product, 0.0).astype(jnp.bfloat16)


def make_own(recorded, v_factors, ranks):
    return pl.pallas_call(
        own_kernel,
        in_specs=[
            pl.BlockSpec(memory_space=pl.ANY),
            pl.BlockSpec(memory_space=pltpu.VMEM),
            pl.BlockSpec(memory_space=pl.ANY),
        ],
        out_specs=pl.BlockSpec(memory_space=pltpu.VMEM),
        out_shape=jax.ShapeDtypeStruct((128, 256), jnp.bfloat16),
        scratch_shapes=[
            pltpu.SMEM(ranks.shape, jnp.int32),
            pltpu.VMEM((2, 2, 256, 128), jnp.bfloat16),
            pltpu.VMEM((2, 512, 256), jnp.bfloat16),
            pltpu.SemaphoreType.DMA((3,)),
        ],
        compiler_params=params(8),
        cost_estimate=pl.CostEstimate(
            flops=2 * 10**8, bytes_accessed=10**6, transcendentals=0
        ),
        name="own",
    )(ranks, recorded, v_factors)


def pack_kernel(u_ref, packed_ref, own_ref, wide_ref):
    rows = u_ref.shape[2]
    column = lax.axis_index("space")
    wide_ref[...] = u_ref[0, 0].reshape(rows * 32, 128).astype(jnp.float32)
    low_lanes = lane_index((rows, 128)) < 64
    for m in range(16):
        even = wide_ref[pl.ds(2 * m, rows, stride=32), :]
        odd = wide_ref[pl.ds(2 * m + 1, rows, stride=32), :]
        both = jnp.where(low_lanes, even, pltpu.roll(odd, 64, 1))
        packed_ref[0, :, m * 128 : (m + 1) * 128] = both.astype(jnp.bfloat16)
    own = wide_ref[pl.ds(column, rows, stride=32), :]
    own_ref[0] = pltpu.roll(own, 64, 1).astype(jnp.bfloat16)


def pack_factors(u_factors, rows=128):
    halves = 256 // rows
    return pl.pallas_call(
        pack_kernel,
        grid=(2, 2, halves),
        in_specs=[pl.BlockSpec((1, 1, rows, 32, 128), lambda f, c, h: (f, c, h, 0, 0))],
        out_specs=[
            pl.BlockSpec((1, rows, 2048), lambda f, c, h: (f, c * halves + h, 0)),
            pl.BlockSpec((1, rows, 128), lambda f, c, h: (f, c * halves + h, 0)),
        ],
        out_shape=[
            jax.ShapeDtypeStruct((2, 512, 2048), jnp.bfloat16),
            jax.ShapeDtypeStruct((2, 512, 128), jnp.bfloat16),
        ],
        scratch_shapes=[pltpu.VMEM((rows * 32, 128), jnp.float32)],
        compiler_params=params(16),
        cost_estimate=pl.CostEstimate(
            flops=10**6, bytes_accessed=40 * 10**6, transcendentals=0
        ),
        name="pack",
    )(u_factors)


def spectra_kernel(packed_ref, own_ref, received_ref, high_ref, *out_refs):
    group = lax.axis_index("freq")
    lane_part = lane_index((64, 128)) // 32
    for f in range(2):
        part = slice(f * 64, (f + 1) * 64)
        total = jnp.dot(
            packed_ref[f],
            received_ref[:, part, :].reshape(2048, 256),
            preferred_element_type=jnp.float32,
        ) + jnp.dot(own_ref[f, :, 0:64], high_ref[part], preferred_element_type=jnp.float32)
        real = total[0:256, 0:128] - total[256:512, 128:256]
        imag = total[0:256, 128:256] + total[256:512, 0:128]
        for c, value in enumerate((real, imag)):
            for m, out_ref in enumerate(out_refs):
                target = group ^ m
                message = jnp.zeros((64, 128), jnp.float32)
                for q in range(4):
                    moved = pltpu.roll(value[q * 64 : (q + 1) * 64], (q + 4 - target) % 4 * 32, 1)
                    message = jnp.where(lane_part == q, moved, message)
                out_ref[2 * f + c] = message.astype(jnp.bfloat16)


def make_spectra(packed, own, received, high):
    message = jax.ShapeDtypeStruct((4, 64, 128), jnp.bfloat16)
    return pl.pallas_call(
        spectra_kernel,
        in_specs=[pl.BlockSpec(memory_space=pltpu.VMEM)] * 4,
        out_specs=[pl.BlockSpec(memory_space=pltpu.VMEM)] * 4,
        out_shape=[message] * 4,
        compiler_params=params(16),
        cost_estimate=pl.CostEstimate(
            flops=2 * 10**9, bytes_accessed=7 * 10**6, transcendentals=0
        ),
        name="spectra",
    )(packed, own, received, high)


def traces_kernel(m0, m1, m2, m3, mute_ref, basis_ref, spread_ref, out_ref, left_ref, start_ref):
    step = pl.program_id(0)

    @pl.when(step == 0)
    def _():
        wide = jnp.concatenate([m[...].astype(jnp.float32) for m in (m0, m1, m2, m3)], axis=0)
        for r in range(8):
            part = wide[:, r * 8 : (r + 1) * 8].reshape(128, 128).T.astype(jnp.bfloat16)
            left_ref[r * 128 : (r + 1) * 128, 0:128] = part
            left_ref[r * 128 : (r + 1) * 128, 128:256] = part
            start = mute_ref[r * 8 : (r + 1) * 8, :].astype(jnp.float32)
            start = jnp.concatenate([start, jnp.zeros((120, 128), jnp.float32)], axis=0)
            start_ref[r * 128 : (r + 1) * 128, :] = start.T.astype(jnp.bfloat16)

    traces = jnp.dot(left_ref[...], basis_ref[...], preferred_element_type=jnp.float32)
    start = jnp.dot(start_ref[...], spread_ref[...], preferred_element_type=jnp.float32)
    times = lane_index((8, 4, 32, 128)).astype(jnp.float32)
    for p in range(2):
        lanes = slice(p * 128, (p + 1) * 128)
        value = traces[:, lanes].reshape(8, 4, 32, 128)
        kept = times >= start[:, lanes].reshape(8, 4, 32, 128)
        value = jnp.where(kept, value, 0.0)
        for q in range(4):
            out_ref[q, :, p] = value[:, q]


def make_traces(messages, mute, basis, spread):
    message = pl.BlockSpec((4, 64, 128), lambda s: (0, 0, 0))
    return pl.pallas_call(
        traces_kernel,
        grid=(4,),
        in_specs=[message] * 4
        + [
            pl.BlockSpec((64, 128), lambda s: (0, 0)),
            pl.BlockSpec((256, 256), lambda s: (0, s)),
            pl.BlockSpec((128, 256), lambda s: (0, s)),
        ],
        out_specs=pl.BlockSpec((4, 8, 2, 32, 128), lambda s: (0, 0, s, 0, 0)),
        out_shape=jax.ShapeDtypeStruct((4, 8, 8, 32, 128), jnp.float32),
        scratch_shapes=[
            pltpu.VMEM((1024, 256), jnp.bfloat16),
            pltpu.VMEM((1024, 128), jnp.bfloat16),
        ],
        compiler_params=params(32),
        cost_estimate=pl.CostEstimate(
            flops=2 * 10**9, bytes_accessed=6 * 10**6, transcendentals=0
        ),
        name="traces",
    )(*messages, mute, basis, spread)


def time_table(freq_total):
    weights = 1 + np.arange(freq_total) * (NT // 2 // freq_total)
    phase = (weights[:, None] * np.arange(NT)[None, :] % NT) * (2.0 * math.pi / NT)
    scale = 1.0 / math.sqrt(2.0 * freq_total)
    table = np.stack([np.cos(phase) * scale, -np.sin(phase) * scale], axis=1)
    return table.astype(np.float32)


def time_operands(group):
    table = time_table(8)
    top = table.astype(jnp.bfloat16)
    rest = (table - top.astype(np.float32)).astype(jnp.bfloat16)
    both = jnp.asarray(np.stack([top, rest])).reshape(2, 4, 4, NT)
    rows = jnp.take(both, group ^ jnp.arange(4, dtype=jnp.int32), axis=1).reshape(2, 16, NT)
    same = jnp.eye(8, dtype=jnp.bfloat16)
    basis = (rows[:, :, None, None, :] * same[None, None, :, :, None]).reshape(256, 8 * NT)
    spread = np.zeros((128, 8, NT), np.float32)
    for p in range(8):
        spread[p, p] = 1.0
    return basis, jnp.asarray(spread.reshape(128, 8 * NT), dtype=jnp.bfloat16)


def shards(recorded, v_factors, u_factors, tile_ranks, mute_start):
    ranks = tile_ranks.reshape(2 * tile_ranks.shape[1], tile_ranks.shape[2])
    send = make_blocks(recorded, v_factors, ranks)
    received = lax.all_to_all(send, "space", split_axis=0, concat_axis=0, tiled=True)
    high = make_own(recorded, v_factors, ranks)
    packed, own = pack_factors(u_factors)
    basis, spread = time_operands(lax.axis_index("freq"))
    mute = mute_start.reshape(4, 64, 32).transpose(1, 0, 2).reshape(64, 128)
    messages = make_spectra(packed, own, received, high)
    arrived = [messages[0]]
    for m in range(1, 4):
        pairs = [(z, z ^ m) for z in range(4)]
        arrived.append(lax.ppermute(messages[m], "freq", pairs))
    traces = make_traces(arrived, mute, basis, spread)
    return traces.reshape(256, 32, NT)


def solution(mesh):
    placed = (
        P("freq", None, "space", None),
        P("freq", None, None, "space", None),
        P("freq", None, "space", None, None),
        P("freq", None, None),
        P("space", "freq"),
    )
    return jax.shard_map(
        shards, mesh=mesh, in_specs=placed, out_specs=P("space", "freq", None), check_vma=False
    )
```

time: 72.9 us -> 61.8 us (0.85)
  Pallas kernels: 0 us -> 26 us
  local copies, waits for them, and re-layouts: 24.8 us -> 6.9 us
  matrix products: 12.5 us -> 0 us
  waiting for transfers between devices: 20.6 us -> 15 us
  other arithmetic: 1.35 us -> 0.21 us
    pallas_call x0 -> x5, Pallas kernels: none -> 26 us  [the longest x1 12.8 us: pack_factors(): pl.pallas_call(pack_kernel, grid=(2, 2, halves), in_specs=[pl.BlockSpec((...]
    dot_general x6 -> x0, matrix products: 12.5 us -> none  [the longest x1 5.33 us: shards(): jnp.einsum('fiak,fabs->fikbs', low_factors, stacked, preferred_element_ty...]
    all_to_all x2 -> x1, waiting for transfers between devices: 20.6 us -> 9.86 us  [shards(): lax.all_to_all(send, 'space', split_axis=0, concat_axis=0, tiled=True)]
    unnamed x11 -> x18, local copies, waits for them, and re-layouts: 12.4 us -> 5.99 us
    ppermute x0 -> x3, starting transfers between devices: none -> 5.66 us  [shards(): arrived.append(lax.ppermute(messages[m], 'freq', pairs))]
    ppermute x0 -> x3, waiting for transfers between devices: none -> 5.17 us  [shards(): arrived.append(lax.ppermute(messages[m], 'freq', pairs))]
    all_to_all x2 -> x1, starting transfers between devices: 12.7 us -> 7.55 us  [shards(): lax.all_to_all(send, 'space', split_axis=0, concat_axis=0, tiled=True)]
    select_n x1 -> x0, local copies, waits for them, and re-layouts: 4.44 us -> none  [shards(): jnp.where(times[None, None, :] >= mute_start[:, :, None], traces, 0.0)]
  transfers between devices with their start and end apart: 2 -> 4, of which waited for: 2 -> 3; matrix products, arithmetic and copies ran while one was open for 21% -> 2% of each run, Pallas kernels for 0% -> 23%
where the time goes in v1:
time: 61.8 us; the launch traced here: 61.5 us
  Pallas kernels  26 us (42%)
  waiting for transfers between devices  15 us (24%)
  starting transfers between devices  13.2 us (21%)
  local copies, waits for them, and re-layouts  6.9 us (11%)
    pallas_call x1, Pallas kernels, pack_factors(): pl.pallas_call(pack_kernel, grid=(2, 2, halves), in_specs=[pl.BlockSpec((...  12.8 us
    all_to_all x1, waiting for transfers between devices, shards(): lax.all_to_all(send, 'space', split_axis=0, concat_axis=0, tiled=True)  9.86 us
    all_to_all x1, starting transfers between devices, shards(): lax.all_to_all(send, 'space', split_axis=0, concat_axis=0, tiled=True)  7.55 us
    pallas_call x1, Pallas kernels, make_blocks(): pl.pallas_call(blocks_kernel, in_specs=[pl.BlockSpec(memory_space=pl.ANY)...  6.44 us
    unnamed x18, local copies, waits for them, and re-layouts  5.99 us
    ppermute x3, starting transfers between devices, shards(): arrived.append(lax.ppermute(messages[m], 'freq', pairs))  5.66 us
    ppermute x3, waiting for transfers between devices, shards(): arrived.append(lax.ppermute(messages[m], 'freq', pairs))  5.17 us
    pallas_call x1, Pallas kernels, make_traces(): pl.pallas_call(traces_kernel, grid=(4,), in_specs=[message] * 4 + [pl.Blo...  3.56 us
  transfers between devices with their start and end apart: 4, of which 3 were waited for; matrix products, arithmetic and copies ran while one was open for 2% of the time, Pallas kernels for 23%

profile of v1, /device:TPU:0, one launch (start us, length us, event | category | flops | bytes accessed | tf_op | source)
XLA Modules:
  0.0 61.5 jit_solution(3298422851175241741)
XLA Ops:
  0.0 6.4 %blocks.1 = bf16[32,128,256]{2,1,0:T(8,128)(2,1)} custom-call(s32[64,32]{1,0:T(8,128)} %bitcast.13, bf16[2,2,256,128]{3,2,1,0:T(8,128)(2,1)} %recorded_ref.1, bf16[2,32,2,256,128]{4,3,2,1,0:T(8,128)(2,1)} %v_hbm.3), custom_call_target="tpu_custom_call" | custom-call | flops 4000000000 | bytes 11000000 | tf_op jit(solution)/shard_map/blocks/pallas_call | solution.py:111
  6.4 0.0 copy-start.8
  6.5 7.5 %all-to-all-start = ((bf16[32,128,256]{2,1,0:T(8,128)(2,1)}), bf16[32,128,256]{2,1,0:T(8,128)(2,1)S(1)}, u32[]{:S(2)}, u32[]{:S(2)}) async-start(bf16[32,128,256]{2,1,0:T(8,128)(2,1)} %blocks.1), calls=%async_computation | async-start | bytes 4194304 | tf_op jit(solution)/shard_map/all_to_all | solution.py:327
  14.1 0.1 broadcast_in_dim.15
  14.1 0.1 broadcast_in_dim.16
  14.2 0.6 gather_fusion
  14.8 3.4 %copy-done = bf16[2,2,256,32,128]{4,3,2,1,0:T(8,128)(2,1)S(1)} copy-done((bf16[2,2,256,32,128]{4,3,2,1,0:T(8,128)(2,1)S(1)}, bf16[2,2,256,32,128]{4,3,2,1,0:T(8,128)(2,1)}, u32[]{:S(2)}) %copy-start) | copy-done | bytes 8388632
  18.2 12.8 %pack.1 = (bf16[2,512,2048]{2,1,0:T(8,128)(2,1)S(1)}, bf16[2,512,128]{2,1,0:T(8,128)(2,1)S(1)}) custom-call(bf16[2,2,256,32,128]{4,3,2,1,0:T(8,128)(2,1)S(1)} %copy-done), custom_call_target="tpu_custom_call" | custom-call | flops 1000000 | bytes 40000000 | tf_op jit(solution)/shard_map/pack/pallas_call | solution.py:193
  31.0 0.0 copy-start.6
  31.0 1.6 %own.1.high_ref = bf16[128,256]{1,0:T(8,128)(2,1)S(1)} custom-call(s32[64,32]{1,0:T(8,128)S(1)} %bitcast.14, bf16[2,2,256,128]{3,2,1,0:T(8,128)(2,1)S(1)} %copy-done.2, bf16[2,32,2,256,128]{4,3,2,1,0:T(8,128)(2,1)S(1)} %copy-done.1), custom_call_target="tpu_custom_call" | custom-call | flops 200000000 | bytes 1000000 | tf_op jit(solution)/shard_map/own/pallas_call | solution.py:154
  32.6 0.4 copy-done.4
  33.0 0.1 broadcast_select_fusion
  33.1 9.9 %all-to-all-done.received_ref = bf16[32,128,256]{2,1,0:T(8,128)(2,1)S(1)} async-done(((bf16[32,128,256]{2,1,0:T(8,128)(2,1)}), bf16[32,128,256]{2,1,0:T(8,128)(2,1)S(1)}, u32[]{:S(2)}, u32[]{:S(2)}) %all-to-all-start) | async-done | bytes 2097184 | tf_op jit(solution)/shard_map/all_to_all | solution.py:327
  43.0 2.2 %copy-done.5 = bf16[2,512,2048]{2,1,0:T(8,128)(2,1)S(1)} copy-done((bf16[2,512,2048]{2,1,0:T(8,128)(2,1)S(1)}, bf16[2,512,2048]{2,1,0:T(8,128)(2,1)}, u32[]{:S(2)}) %copy-start.5) | copy-done | bytes 4194328
  45.2 1.6 %spectra.1 = (bf16[4,64,128]{2,1,0:T(8,128)(2,1)S(1)}, bf16[4,64,128]{2,1,0:T(8,128)(2,1)S(1)}, bf16[4,64,128]{2,1,0:T(8,128)(2,1)S(1)}, bf16[4,64,128]{2,1,0:T(8,128)(2,1)S(1)}) custom-call(bf16[2,512,2048]{2,1,0:T(8,128)(2,1)S(1)} %copy-done.5, bf16[2,512,128]{2,1,0:T(8,128)(2,1)S(1)} %get-tuple-element.12.own_ref, ...), custom_call_target="tpu_custom_call" | custom-call | flops 2000000000 | bytes 7000000 | tf_op jit(solution)/shard_map/spectra/pallas_call | solution.py:238
  46.8 2.0 %collective-permute-start = (bf16[4,64,128]{2,1,0:T(8,128)(2,1)S(1)}, bf16[4,64,128]{2,1,0:T(8,128)(2,1)S(1)}, u32[]{:S(2)}, u32[]{:S(2)}) collective-permute-start(bf16[4,64,128]{2,1,0:T(8,128)(2,1)S(1)} %get-tuple-element.14), channel_id=1, source_target_pairs={{0,32},{32,0},{64,96},{96,64},{1,33},{33,1},{65,97},{97,65},{2,34}... | collective-permute-start | bytes 196616 | tf_op jit(solution)/shard_map/ppermute | solution.py:336
  48.8 3.7 %collective-permute-start.1 = (bf16[4,64,128]{2,1,0:T(8,128)(2,1)S(1)}, bf16[4,64,128]{2,1,0:T(8,128)(2,1)S(1)}, u32[]{:S(2)}, u32[]{:S(2)}) collective-permute-start(bf16[4,64,128]{2,1,0:T(8,128)(2,1)S(1)} %get-tuple-element.15), channel_id=1, source_target_pairs={{0,64},{32,96},{64,0},{96,32},{1,65},{33,97},{65,1},{97,33},{2,66}... | collective-permute-start | bytes 196616 | tf_op jit(solution)/shard_map/ppermute | solution.py:336
  52.5 0.1 broadcast_multiply_fusion
  52.6 0.1 reshape.55
  52.7 0.1 copy.13.mute_ref
  52.8 0.0 collective-permute-done.m1
  52.8 2.7 %collective-permute-done.1.m2 = bf16[4,64,128]{2,1,0:T(8,128)(2,1)S(1)} collective-permute-done((bf16[4,64,128]{2,1,0:T(8,128)(2,1)S(1)}, bf16[4,64,128]{2,1,0:T(8,128)(2,1)S(1)}, u32[]{:S(2)}, u32[]{:S(2)}) %collective-permute-start.1) | collective-permute-done | bytes 65568 | tf_op jit(solution)/shard_map/ppermute | solution.py:336
  55.5 2.4 %collective-permute-done.2.m3 = bf16[4,64,128]{2,1,0:T(8,128)(2,1)S(1)} collective-permute-done((bf16[4,64,128]{2,1,0:T(8,128)(2,1)S(1)}, bf16[4,64,128]{2,1,0:T(8,128)(2,1)S(1)}, u32[]{:S(2)}, u32[]{:S(2)}) %collective-permute-start.2) | collective-permute-done | bytes 65568 | tf_op jit(solution)/shard_map/ppermute | solution.py:336
  57.9 3.6 %traces.1 = f32[4,8,8,32,128]{4,3,2,1,0:T(8,128)} custom-call(bf16[4,64,128]{2,1,0:T(8,128)(2,1)S(1)} %get-tuple-element.13.m0, bf16[4,64,128]{2,1,0:T(8,128)(2,1)S(1)} %collective-permute-done.m1, bf16[4,64,128]{2,1,0:T(8,128)(2,1)S(1)} %collective-permute-done.1.m2, bf16[4,64,128]{2,1,0:T(8,128)(2,1)S(1)} %collective-permute-done.2.m3, ...), custom_call_target="tpu_custom_call" | custom-call | flops 2000000000 | bytes 6000000 | tf_op jit(solution)/shard_map/traces/pallas_call | solution.py:279
  (20 shorter events, 0.1 us)
Async XLA Ops:
  6.4 7.8 %copy-start.8 = (bf16[2,4,4,128]{3,2,1,0:T(4,128)(2,1)S(1)}, bf16[2,4,4,128]{3,2,1,0:T(4,128)(2,1)}, u32[]{:S(2)}) copy-start(bf16[2,4,4,128]{3,2,1,0:T(4,128)(2,1)} %constant.32) | copy-start | bytes 24580
  6.5 24.5 %copy-start.2 = (bf16[2,2,256,128]{3,2,1,0:T(8,128)(2,1)S(1)}, bf16[2,2,256,128]{3,2,1,0:T(8,128)(2,1)}, u32[]{:S(2)}) copy-start(bf16[2,2,256,128]{3,2,1,0:T(8,128)(2,1)} %recorded_ref.1) | copy-start | bytes 786436
  6.5 24.5 %copy-start.3 = (s32[2,32,32]{2,1,0:T(8,128)S(1)}, s32[2,32,32]{2,1,0:T(8,128)}, u32[]{:S(2)}) copy-start(s32[2,32,32]{2,1,0:T(8,128)} %param.10) | copy-start | bytes 24580
  6.5 36.5 %all-to-all-start = ((bf16[32,128,256]{2,1,0:T(8,128)(2,1)}), bf16[32,128,256]{2,1,0:T(8,128)(2,1)S(1)}, u32[]{:S(2)}, u32[]{:S(2)}) async-start(bf16[32,128,256]{2,1,0:T(8,128)(2,1)} %blocks.1), calls=%async_computation | async-start | bytes 4194304 | tf_op jit(solution)/shard_map/all_to_all | solution.py:327
  14.8 3.4 %copy-start = (bf16[2,2,256,32,128]{4,3,2,1,0:T(8,128)(2,1)S(1)}, bf16[2,2,256,32,128]{4,3,2,1,0:T(8,128)(2,1)}, u32[]{:S(2)}) copy-start(bf16[2,2,256,32,128]{4,3,2,1,0:T(8,128)(2,1)} %u_ref.1) | copy-start | bytes 25165828
  18.2 12.8 %copy-start.1 = (bf16[2,32,2,256,128]{4,3,2,1,0:T(8,128)(2,1)S(1)}, bf16[2,32,2,256,128]{4,3,2,1,0:T(8,128)(2,1)}, u32[]{:S(2)}) copy-start(bf16[2,32,2,256,128]{4,3,2,1,0:T(8,128)(2,1)} %v_hbm.3) | copy-start | bytes 25165828
  31.0 2.0 %copy-start.4 = (bf16[2,512,2048]{2,1,0:T(8,128)(2,1)}, bf16[2,512,2048]{2,1,0:T(8,128)(2,1)S(1)}, u32[]{:S(2)}) copy-start(bf16[2,512,2048]{2,1,0:T(8,128)(2,1)S(1)} %get-tuple-element.11.packed_ref) | copy-start | bytes 12582916
  31.0 21.6 %copy-start.7 = (s32[256,32]{0,1:T(8,128)S(1)}, s32[256,32]{0,1:T(8,128)}, u32[]{:S(2)}) copy-start(s32[256,32]{0,1:T(8,128)} %param.11) | copy-start | bytes 98308
  31.0 26.9 %copy-start.6 = (bf16[128,1024]{1,0:T(8,128)(2,1)S(1)}, bf16[128,1024]{1,0:T(8,128)(2,1)}, u32[]{:S(2)}) copy-start(bf16[128,1024]{1,0:T(8,128)(2,1)} %constant.27.clone.spread_ref) | copy-start | bytes 786436
  43.0 2.2 %copy-start.5 = (bf16[2,512,2048]{2,1,0:T(8,128)(2,1)S(1)}, bf16[2,512,2048]{2,1,0:T(8,128)(2,1)}, u32[]{:S(2)}) copy-start(bf16[2,512,2048]{2,1,0:T(8,128)(2,1)} %copy-done.4) | copy-start | bytes 12582916
  46.8 6.0 %collective-permute-start = (bf16[4,64,128]{2,1,0:T(8,128)(2,1)S(1)}, bf16[4,64,128]{2,1,0:T(8,128)(2,1)S(1)}, u32[]{:S(2)}, u32[]{:S(2)}) collective-permute-start(bf16[4,64,128]{2,1,0:T(8,128)(2,1)S(1)} %get-tuple-element.14), channel_id=1, source_target_pairs={{0,32},{32,0},{64,96},{96,64},{1,33},{33,1},{65,97},{97,65},{2,34}... | collective-permute-start | bytes 196616 | tf_op jit(solution)/shard_map/ppermute | solution.py:336
  48.8 6.7 %collective-permute-start.1 = (bf16[4,64,128]{2,1,0:T(8,128)(2,1)S(1)}, bf16[4,64,128]{2,1,0:T(8,128)(2,1)S(1)}, u32[]{:S(2)}, u32[]{:S(2)}) collective-permute-start(bf16[4,64,128]{2,1,0:T(8,128)(2,1)S(1)} %get-tuple-element.15), channel_id=1, source_target_pairs={{0,64},{32,96},{64,0},{96,32},{1,65},{33,97},{65,1},{97,33},{2,66}... | collective-permute-start | bytes 196616 | tf_op jit(solution)/shard_map/ppermute | solution.py:336
  52.5 5.5 %collective-permute-start.2 = (bf16[4,64,128]{2,1,0:T(8,128)(2,1)S(1)}, bf16[4,64,128]{2,1,0:T(8,128)(2,1)S(1)}, u32[]{:S(2)}, u32[]{:S(2)}) collective-permute-start(bf16[4,64,128]{2,1,0:T(8,128)(2,1)S(1)} %get-tuple-element.16), channel_id=1, source_target_pairs={{0,96},{32,64},{64,32},{96,0},{1,97},{33,65},{65,33},{97,1},{2,98}... | collective-permute-start | bytes 196616 | tf_op jit(solution)/shard_map/ppermute | solution.py:336

commit v2 on v1

--- a/solution.py
+++ b/solution.py
@@ -43,85 +43,109 @@
     )
 
 
+GROUP = 8
+
+
+def order_tiles(order, rank_of, count):
+    def place(i, n):
+        some = rank_of(i) > 0
+        order[jnp.where(some, n, count - 1 - (i - n))] = i
+        return n + some.astype(jnp.int32)
+
+    return lax.fori_loop(0, count, place, jnp.int32(0))
+
+
 def blocks_kernel(
     ranks_hbm, recorded_hbm, v_hbm, send_hbm,
-    ranks, recorded, stacked, factors, blocks, small_sem, v_sem, send_sem,
+    ranks, order, recorded, stacked, factors, blocks, empty, small_sem, v_sem, send_sem,
 ):
     column = lax.axis_index("space")
     tile_count = factors.shape[1]
-    parts = send_sem.shape[0]
-    width = tile_count // parts
     get_ranks = pltpu.make_async_copy(ranks_hbm, ranks, small_sem.at[0])
     get_recorded = pltpu.make_async_copy(recorded_hbm, recorded, small_sem.at[1])
     get_ranks.start()
     get_recorded.start()
+    empty[...] = jnp.zeros_like(empty)
 
     def get_tile(f, i):
         return pltpu.make_async_copy(v_hbm.at[f, i], factors.at[f, i], v_sem.at[f, i])
 
-    def get_first(f):
-        first = pl.ds(0, width)
-        return pltpu.make_async_copy(v_hbm.at[f, first], factors.at[f, first], v_sem.at[f, 0])
-
-    def put_part(part):
-        rows = pl.ds(part * width, width)
-        return pltpu.make_async_copy(blocks.at[rows], send_hbm.at[rows], send_sem.at[part])
-
-    for f in range(2):
-        get_first(f).start()
+    def slot(f, i):
+        return send_hbm.at[i, pl.ds(f * 64, 64)]
+
+    def put_tile(f, i):
+        return pltpu.make_async_copy(blocks.at[f, i], slot(f, i), send_sem.at[f])
+
+    def put_empty(f, i):
+        return pltpu.make_async_copy(empty, slot(f, i), send_sem.at[f])
+
     get_ranks.wait()
-
-    @pl.loop(width, tile_count)
-    def _(i):
-        for f in range(2):
-
-            @pl.when(ranks[tile_count * f + i, column] > 0)
+    counts = []
+    for f in range(2):
+
+        def rank_of(i, f=f):
+            rank = ranks[tile_count * f + i, column]
+
+            @pl.when(rank > 0)
             def _():
                 get_tile(f, i).start()
+
+            return rank
+
+        counts.append(order_tiles(order.at[f], rank_of, tile_count))
+    groups = [(n + GROUP - 1) // GROUP for n in counts]
+    for f in range(2):
+
+        @pl.loop(groups[f] * GROUP, tile_count)
+        def _(n):
+            put_empty(f, order[f, n]).start()
 
     get_recorded.wait()
     stack_sources(recorded, stacked)
     row = row_index((64, 256))
-    for part in range(parts):
-        if part == 0:
-            for f in range(2):
-                get_first(f).wait()
-        else:
-            for i in range(part * width, (part + 1) * width):
-                for f in range(2):
-
-                    @pl.when(ranks[tile_count * f + i, column] > 0)
-                    def _():
-                        get_tile(f, i).wait()
-
-        for i in range(part * width, (part + 1) * width):
-            for f in range(2):
+    for f in range(2):
+
+        @pl.loop(0, groups[f])
+        def _(g):
+            tiles = [order[f, g * GROUP + t] for t in range(GROUP)]
+            for t, i in enumerate(tiles):
+
+                @pl.when(g * GROUP + t < counts[f])
+                def _():
+                    get_tile(f, i).wait()
+
+            for i in tiles:
                 product = transposed_dot(factors[f, i], stacked[f])[0:64]
                 kept = row < ranks[tile_count * f + i, column]
-                blocks[i, f * 64 : (f + 1) * 64] = jnp.where(kept, product, 0.0).astype(
-                    jnp.bfloat16
-                )
-        put_part(part).start()
-    for part in range(parts):
-        put_part(part).wait()
-
-
-def make_blocks(recorded, v_factors, ranks, parts=4):
+                blocks[f, i] = jnp.where(kept, product, 0.0).astype(jnp.bfloat16)
+            for i in tiles:
+                put_tile(f, i).start()
+
+    for f in range(2):
+
+        @pl.loop(0, tile_count)
+        def _(i):
+            put_tile(f, i).wait()
+
+
+def make_blocks(recorded, v_factors, ranks):
     tile_count = v_factors.shape[1]
     return pl.pallas_call(
         blocks_kernel,
-        in_specs=[pl.BlockSpec(memory_space=pl.ANY)] * 3,
+        in_specs=[pl.BlockSpec(memory_space=pltpu.HBM)] * 3,
         out_specs=pl.BlockSpec(memory_space=pltpu.HBM),
         out_shape=jax.ShapeDtypeStruct((tile_count, 128, 256), jnp.bfloat16),
         scratch_shapes=[
             pltpu.SMEM(ranks.shape, jnp.int32),
+            pltpu.SMEM((2, tile_count), jnp.int32),
             pltpu.VMEM((2, 2, 256, 128), jnp.bfloat16),
             pltpu.VMEM((2, 512, 256), jnp.bfloat16),
             pltpu.VMEM((2, tile_count, 2, 256, 128), jnp.bfloat16),
-            pltpu.VMEM((tile_count, 128, 256), jnp.bfloat16),
+            pltpu.VMEM((2, tile_count, 64, 256), jnp.bfloat16),
+            pltpu.VMEM((64, 256), jnp.bfloat16),
             pltpu.SemaphoreType.DMA((2,)),
             pltpu.SemaphoreType.DMA((2, tile_count)),
-            pltpu.SemaphoreType.DMA((parts,)),
+            pltpu.SemaphoreType.DMA((2,)),
         ],
         compiler_params=params(60),
         cost_estimate=pl.CostEstimate(
@@ -131,84 +155,90 @@
     )(ranks, recorded, v_factors)
 
 
-def own_kernel(ranks_hbm, recorded_ref, v_hbm, high_ref, ranks, factors, stacked, sem):
+def prepare_kernel(
+    ranks_hbm, recorded_hbm, v_hbm, u_hbm, packed_ref, own_ref, high_ref,
+    ranks, recorded, stacked, factors, rows_in, wide, small_sem, u_sem,
+):
     column = lax.axis_index("space")
-    get_ranks = pltpu.make_async_copy(ranks_hbm, ranks, sem.at[0])
-    get_ranks.start()
-    copies = [
-        pltpu.make_async_copy(v_hbm.at[f, column], factors.at[f], sem.at[1 + f]) for f in range(2)
+    tile_count = u_hbm.shape[3]
+    count = rows_in.shape[1]
+    steps = 1024 // count
+    per_component = 256 // count
+
+    def get_rows(step):
+        f = step // (2 * per_component)
+        c = step // per_component % 2
+        rows = pl.ds(step % per_component * count, count)
+        slot = step % 2
+        return pltpu.make_async_copy(u_hbm.at[f, c, rows], rows_in.at[slot], u_sem.at[slot])
+
+    get_rows(0).start()
+    small = [
+        pltpu.make_async_copy(ranks_hbm, ranks, small_sem.at[0]),
+        pltpu.make_async_copy(recorded_hbm, recorded, small_sem.at[1]),
+    ] + [
+        pltpu.make_async_copy(v_hbm.at[f, column], factors.at[f], small_sem.at[2 + f])
+        for f in range(2)
     ]
-    for copy in copies:
+    for copy in small:
         copy.start()
-    stack_sources(recorded_ref, stacked)
-    get_ranks.wait()
+    low_lanes = lane_index((count, 128)) < 64
+
+    @pl.loop(0, steps)
+    def _(step):
+        @pl.when(step + 1 < steps)
+        def _():
+            get_rows(step + 1).start()
+
+        get_rows(step).wait()
+        wide[...] = rows_in[step % 2].reshape(count * tile_count, 128).astype(jnp.float32)
+        f = step // (2 * per_component)
+        rows = pl.ds(pl.multiple_of(step % (2 * per_component) * count, count), count)
+        for m in range(tile_count // 2):
+            even = wide[pl.ds(2 * m, count, stride=tile_count), :]
+            odd = wide[pl.ds(2 * m + 1, count, stride=tile_count), :]
+            both = jnp.where(low_lanes, even, pltpu.roll(odd, 64, 1))
+            packed_ref[f, rows, m * 128 : (m + 1) * 128] = both.astype(jnp.bfloat16)
+        own = wide[pl.ds(column, count, stride=tile_count), :]
+        own_ref[f, rows, :] = pltpu.roll(own, 64, 1).astype(jnp.bfloat16)
+
+    for copy in small:
+        copy.wait()
+    stack_sources(recorded, stacked)
     row = row_index((64, 256)) + 64
     for f in range(2):
-        copies[f].wait()
         product = transposed_dot(factors[f], stacked[f])[64:128]
-        kept = row < ranks[ranks.shape[1] * f + column, column]
+        kept = row < ranks[tile_count * f + column, column]
         high_ref[f * 64 : (f + 1) * 64] = jnp.where(kept, product, 0.0).astype(jnp.bfloat16)
 
 
-def make_own(recorded, v_factors, ranks):
+def prepare(recorded, v_factors, u_factors, ranks, rows=128):
+    tile_count = u_factors.shape[3]
     return pl.pallas_call(
-        own_kernel,
-        in_specs=[
-            pl.BlockSpec(memory_space=pl.ANY),
-            pl.BlockSpec(memory_space=pltpu.VMEM),
-            pl.BlockSpec(memory_space=pl.ANY),
-        ],
-        out_specs=pl.BlockSpec(memory_space=pltpu.VMEM),
-        out_shape=jax.ShapeDtypeStruct((128, 256), jnp.bfloat16),
+        prepare_kernel,
+        in_specs=[pl.BlockSpec(memory_space=pltpu.HBM)] * 4,
+        out_specs=[pl.BlockSpec(memory_space=pltpu.VMEM)] * 3,
+        out_shape=[
+            jax.ShapeDtypeStruct((2, 512, tile_count * 64), jnp.bfloat16),
+            jax.ShapeDtypeStruct((2, 512, 128), jnp.bfloat16),
+            jax.ShapeDtypeStruct((128, 256), jnp.bfloat16),
+        ],
         scratch_shapes=[
             pltpu.SMEM(ranks.shape, jnp.int32),
             pltpu.VMEM((2, 2, 256, 128), jnp.bfloat16),
             pltpu.VMEM((2, 512, 256), jnp.bfloat16),
-            pltpu.SemaphoreType.DMA((3,)),
-        ],
-        compiler_params=params(8),
-        cost_estimate=pl.CostEstimate(
-            flops=2 * 10**8, bytes_accessed=10**6, transcendentals=0
-        ),
-        name="own",
-    )(ranks, recorded, v_factors)
-
-
-def pack_kernel(u_ref, packed_ref, own_ref, wide_ref):
-    rows = u_ref.shape[2]
-    column = lax.axis_index("space")
-    wide_ref[...] = u_ref[0, 0].reshape(rows * 32, 128).astype(jnp.float32)
-    low_lanes = lane_index((rows, 128)) < 64
-    for m in range(16):
-        even = wide_ref[pl.ds(2 * m, rows, stride=32), :]
-        odd = wide_ref[pl.ds(2 * m + 1, rows, stride=32), :]
-        both = jnp.where(low_lanes, even, pltpu.roll(odd, 64, 1))
-        packed_ref[0, :, m * 128 : (m + 1) * 128] = both.astype(jnp.bfloat16)
-    own = wide_ref[pl.ds(column, rows, stride=32), :]
-    own_ref[0] = pltpu.roll(own, 64, 1).astype(jnp.bfloat16)
-
-
-def pack_factors(u_factors, rows=128):
-    halves = 256 // rows
-    return pl.pallas_call(
-        pack_kernel,
-        grid=(2, 2, halves),
-        in_specs=[pl.BlockSpec((1, 1, rows, 32, 128), lambda f, c, h: (f, c, h, 0, 0))],
-        out_specs=[
-            pl.BlockSpec((1, rows, 2048), lambda f, c, h: (f, c * halves + h, 0)),
-            pl.BlockSpec((1, rows, 128), lambda f, c, h: (f, c * halves + h, 0)),
-        ],
-        out_shape=[
-            jax.ShapeDtypeStruct((2, 512, 2048), jnp.bfloat16),
-            jax.ShapeDtypeStruct((2, 512, 128), jnp.bfloat16),
-        ],
-        scratch_shapes=[pltpu.VMEM((rows * 32, 128), jnp.float32)],
+            pltpu.VMEM((2, 2, 256, 128), jnp.bfloat16),
+            pltpu.VMEM((2, rows, tile_count, 128), jnp.bfloat16),
+            pltpu.VMEM((rows * tile_count, 128), jnp.float32),
+            pltpu.SemaphoreType.DMA((4,)),
+            pltpu.SemaphoreType.DMA((2,)),
+        ],
         compiler_params=params(16),
         cost_estimate=pl.CostEstimate(
-            flops=10**6, bytes_accessed=40 * 10**6, transcendentals=0
+            flops=2 * 10**8, bytes_accessed=40 * 10**6, transcendentals=0
         ),
-        name="pack",
-    )(u_factors)
+        name="prepare",
+    )(ranks, recorded, v_factors, u_factors)
 
 
 def spectra_kernel(packed_ref, own_ref, received_ref, high_ref, *out_refs):
@@ -265,7 +295,7 @@
     traces = jnp.dot(left_ref[...], basis_ref[...], preferred_element_type=jnp.float32)
     start = jnp.dot(start_ref[...], spread_ref[...], preferred_element_type=jnp.float32)
     times = lane_index((8, 4, 32, 128)).astype(jnp.float32)
-    for p in range(2):
+    for p in range(out_ref.shape[2]):
         lanes = slice(p * 128, (p + 1) * 128)
         value = traces[:, lanes].reshape(8, 4, 32, 128)
         kept = times >= start[:, lanes].reshape(8, 4, 32, 128)
@@ -274,18 +304,18 @@
             out_ref[q, :, p] = value[:, q]
 
 
-def make_traces(messages, mute, basis, spread):
+def make_traces(messages, mute, basis, spread, width=4):
     message = pl.BlockSpec((4, 64, 128), lambda s: (0, 0, 0))
     return pl.pallas_call(
         traces_kernel,
-        grid=(4,),
+        grid=(8 // width,),
         in_specs=[message] * 4
         + [
             pl.BlockSpec((64, 128), lambda s: (0, 0)),
-            pl.BlockSpec((256, 256), lambda s: (0, s)),
-            pl.BlockSpec((128, 256), lambda s: (0, s)),
-        ],
-        out_specs=pl.BlockSpec((4, 8, 2, 32, 128), lambda s: (0, 0, s, 0, 0)),
+            pl.BlockSpec((256, width * NT), lambda s: (0, s)),
+            pl.BlockSpec((128, width * NT), lambda s: (0, s)),
+        ],
+        out_specs=pl.BlockSpec((4, 8, width, 32, NT), lambda s: (0, 0, s, 0, 0)),
         out_shape=jax.ShapeDtypeStruct((4, 8, 8, 32, 128), jnp.float32),
         scratch_shapes=[
             pltpu.VMEM((1024, 256), jnp.bfloat16),
@@ -325,8 +355,7 @@
     ranks = tile_ranks.reshape(2 * tile_ranks.shape[1], tile_ranks.shape[2])
     send = make_blocks(recorded, v_factors, ranks)
     received = lax.all_to_all(send, "space", split_axis=0, concat_axis=0, tiled=True)
-    high = make_own(recorded, v_factors, ranks)
-    packed, own = pack_factors(u_factors)
+    packed, own, high = prepare(recorded, v_factors, u_factors, ranks)
     basis, spread = time_operands(lax.axis_index("freq"))
     mute = mute_start.reshape(4, 64, 32).transpose(1, 0, 2).reshape(64, 128)
     messages = make_spectra(packed, own, received, high)

time: 61.8 us -> 61.1 us (0.989)
  local copies, waits for them, and re-layouts: 6.9 us -> 11.9 us
  waiting for transfers between devices: 15 us -> 10.2 us
  Pallas kernels: 26 us -> 24.7 us
    unnamed x18, local copies, waits for them, and re-layouts: 5.99 us -> 11 us
    all_to_all x1, waiting for transfers between devices: 9.86 us -> 5.04 us  [shards(): lax.all_to_all(send, 'space', split_axis=0, concat_axis=0, tiled=True)]
    pallas_call x4 -> x3, Pallas kernels: 24.3 us -> 23 us  [the longest x1 14.2 us: prepare(): pl.pallas_call(prepare_kernel, in_specs=[pl.BlockSpec(memory_space=pltpu....]
where the time goes in v2:
time: 61.1 us; the launch traced here: 60.8 us
  Pallas kernels  24.7 us (40%)
  starting transfers between devices  13.6 us (22%)
  local copies, waits for them, and re-layouts  11.9 us (19%)
  waiting for transfers between devices  10.2 us (17%)
    pallas_call x1, Pallas kernels, prepare(): pl.pallas_call(prepare_kernel, in_specs=[pl.BlockSpec(memory_space=pltpu....  14.2 us
    unnamed x18, local copies, waits for them, and re-layouts  11 us
    all_to_all x1, starting transfers between devices, shards(): lax.all_to_all(send, 'space', split_axis=0, concat_axis=0, tiled=True)  7.99 us
    pallas_call x1, Pallas kernels, make_blocks(): pl.pallas_call(blocks_kernel, in_specs=[pl.BlockSpec(memory_space=pltpu.H...  5.81 us
    ppermute x3, starting transfers between devices, shards(): arrived.append(lax.ppermute(messages[m], 'freq', pairs))  5.63 us
    ppermute x3, waiting for transfers between devices, shards(): arrived.append(lax.ppermute(messages[m], 'freq', pairs))  5.17 us
    all_to_all x1, waiting for transfers between devices, shards(): lax.all_to_all(send, 'space', split_axis=0, concat_axis=0, tiled=True)  5.04 us
    pallas_call x1, Pallas kernels, make_traces(): pl.pallas_call(traces_kernel, grid=(8 // width,), in_specs=[message] * 4...  3.03 us
  transfers between devices with their start and end apart: 4, of which 3 were waited for; matrix products, arithmetic and copies ran while one was open for 2% of the time, Pallas kernels for 23%

profile of v2, /device:TPU:0, one launch (start us, length us, event | category | flops | bytes accessed | tf_op | source)
XLA Modules:
  0.0 60.8 jit_solution(3914447702160324013)
XLA Ops:
  0.0 5.8 %blocks.1 = bf16[32,128,256]{2,1,0:T(8,128)(2,1)} custom-call(s32[64,32]{1,0:T(8,128)} %bitcast.13, bf16[2,2,256,128]{3,2,1,0:T(8,128)(2,1)} %recorded_hbm.3, bf16[2,32,2,256,128]{4,3,2,1,0:T(8,128)(2,1)} %v_hbm.3), custom_call_target="tpu_custom_call" | custom-call | flops 4000000000 | bytes 11000000 | tf_op jit(solution)/shard_map/blocks/pallas_call | solution.py:133
  5.8 0.0 copy-start.8
  5.8 0.0 copy-start.2
  5.9 8.0 %all-to-all-start = ((bf16[32,128,256]{2,1,0:T(8,128)(2,1)}), bf16[32,128,256]{2,1,0:T(8,128)(2,1)S(1)}, u32[]{:S(2)}, u32[]{:S(2)}) async-start(bf16[32,128,256]{2,1,0:T(8,128)(2,1)} %blocks.1), calls=%async_computation | async-start | bytes 4194304 | tf_op jit(solution)/shard_map/all_to_all | solution.py:357
  13.9 0.1 broadcast_in_dim.15
  14.0 0.1 broadcast_in_dim.16
  14.1 0.6 gather_fusion
  14.7 3.4 %copy-done = bf16[2,32,2,256,128]{4,3,2,1,0:T(8,128)(2,1)S(1)} copy-done((bf16[2,32,2,256,128]{4,3,2,1,0:T(8,128)(2,1)S(1)}, bf16[2,32,2,256,128]{4,3,2,1,0:T(8,128)(2,1)}, u32[]{:S(2)}) %copy-start) | copy-done | bytes 8388632
  18.1 3.4 %copy-done.1 = bf16[2,2,256,32,128]{4,3,2,1,0:T(8,128)(2,1)S(1)} copy-done((bf16[2,2,256,32,128]{4,3,2,1,0:T(8,128)(2,1)S(1)}, bf16[2,2,256,32,128]{4,3,2,1,0:T(8,128)(2,1)}, u32[]{:S(2)}) %copy-start.1) | copy-done | bytes 8388632
  21.4 14.2 %prepare.1 = (bf16[2,512,2048]{2,1,0:T(8,128)(2,1)S(1)}, bf16[2,512,128]{2,1,0:T(8,128)(2,1)S(1)}, bf16[128,256]{1,0:T(8,128)(2,1)S(1)}) custom-call(s32[64,32]{1,0:T(8,128)S(1)} %bitcast.14, bf16[2,2,256,128]{3,2,1,0:T(8,128)(2,1)S(1)} %copy-done.2, bf16[2,32,2,256,128]{4,3,2,1,0:T(8,128)(2,1)S(1)} %copy-done, bf16[2,2,256,32,128]{4,3,2,1,0:T(8,128)(2,1)S(1)} %copy-done.1), custom_call_target="tpu_custom_call" | custom-call | flops 200000000 | bytes 40000000 | tf_op jit(solution)/shard_map/prepare/pallas_call | solution.py:217
  35.7 2.0 %copy-done.4 = bf16[2,512,2048]{2,1,0:T(8,128)(2,1)} copy-done((bf16[2,512,2048]{2,1,0:T(8,128)(2,1)}, bf16[2,512,2048]{2,1,0:T(8,128)(2,1)S(1)}, u32[]{:S(2)}) %copy-start.4) | copy-done | bytes 4194328
  37.7 0.1 broadcast_select_fusion
  37.8 5.0 %all-to-all-done.received_ref = bf16[32,128,256]{2,1,0:T(8,128)(2,1)S(1)} async-done(((bf16[32,128,256]{2,1,0:T(8,128)(2,1)}), bf16[32,128,256]{2,1,0:T(8,128)(2,1)S(1)}, u32[]{:S(2)}, u32[]{:S(2)}) %all-to-all-start) | async-done | bytes 2097184 | tf_op jit(solution)/shard_map/all_to_all | solution.py:357
  42.8 2.2 %copy-done.5 = bf16[2,512,2048]{2,1,0:T(8,128)(2,1)S(1)} copy-done((bf16[2,512,2048]{2,1,0:T(8,128)(2,1)S(1)}, bf16[2,512,2048]{2,1,0:T(8,128)(2,1)}, u32[]{:S(2)}) %copy-start.5) | copy-done | bytes 4194328
  45.0 1.6 %spectra.1 = (bf16[4,64,128]{2,1,0:T(8,128)(2,1)S(1)}, bf16[4,64,128]{2,1,0:T(8,128)(2,1)S(1)}, bf16[4,64,128]{2,1,0:T(8,128)(2,1)S(1)}, bf16[4,64,128]{2,1,0:T(8,128)(2,1)S(1)}) custom-call(bf16[2,512,2048]{2,1,0:T(8,128)(2,1)S(1)} %copy-done.5, bf16[2,512,128]{2,1,0:T(8,128)(2,1)S(1)} %get-tuple-element.13.own_ref, ...), custom_call_target="tpu_custom_call" | custom-call | flops 2000000000 | bytes 7000000 | tf_op jit(solution)/shard_map/spectra/pallas_call | solution.py:268
  46.6 2.0 %collective-permute-start = (bf16[4,64,128]{2,1,0:T(8,128)(2,1)S(1)}, bf16[4,64,128]{2,1,0:T(8,128)(2,1)S(1)}, u32[]{:S(2)}, u32[]{:S(2)}) collective-permute-start(bf16[4,64,128]{2,1,0:T(8,128)(2,1)S(1)} %get-tuple-element.16), channel_id=1, source_target_pairs={{0,32},{32,0},{64,96},{96,64},{1,33},{33,1},{65,97},{97,65},{2,34}... | collective-permute-start | bytes 196616 | tf_op jit(solution)/shard_map/ppermute | solution.py:365
  48.7 3.6 %collective-permute-start.1 = (bf16[4,64,128]{2,1,0:T(8,128)(2,1)S(1)}, bf16[4,64,128]{2,1,0:T(8,128)(2,1)S(1)}, u32[]{:S(2)}, u32[]{:S(2)}) collective-permute-start(bf16[4,64,128]{2,1,0:T(8,128)(2,1)S(1)} %get-tuple-element.17), channel_id=1, source_target_pairs={{0,64},{32,96},{64,0},{96,32},{1,65},{33,97},{65,1},{97,33},{2,66}... | collective-permute-start | bytes 196616 | tf_op jit(solution)/shard_map/ppermute | solution.py:365
  52.3 0.1 broadcast_multiply_fusion
  52.4 0.1 reshape.55
  52.5 0.1 copy.13.mute_ref
  52.6 0.0 collective-permute-done.m1
  52.6 2.7 %collective-permute-done.1.m2 = bf16[4,64,128]{2,1,0:T(8,128)(2,1)S(1)} collective-permute-done((bf16[4,64,128]{2,1,0:T(8,128)(2,1)S(1)}, bf16[4,64,128]{2,1,0:T(8,128)(2,1)S(1)}, u32[]{:S(2)}, u32[]{:S(2)}) %collective-permute-start.1) | collective-permute-done | bytes 65568 | tf_op jit(solution)/shard_map/ppermute | solution.py:365
  55.3 2.4 %collective-permute-done.2.m3 = bf16[4,64,128]{2,1,0:T(8,128)(2,1)S(1)} collective-permute-done((bf16[4,64,128]{2,1,0:T(8,128)(2,1)S(1)}, bf16[4,64,128]{2,1,0:T(8,128)(2,1)S(1)}, u32[]{:S(2)}, u32[]{:S(2)}) %collective-permute-start.2) | collective-permute-done | bytes 65568 | tf_op jit(solution)/shard_map/ppermute | solution.py:365
  57.7 3.0 %traces.1 = f32[4,8,8,32,128]{4,3,2,1,0:T(8,128)} custom-call(bf16[4,64,128]{2,1,0:T(8,128)(2,1)S(1)} %get-tuple-element.15.m0, bf16[4,64,128]{2,1,0:T(8,128)(2,1)S(1)} %collective-permute-done.m1, bf16[4,64,128]{2,1,0:T(8,128)(2,1)S(1)} %collective-permute-done.1.m2, bf16[4,64,128]{2,1,0:T(8,128)(2,1)S(1)} %collective-permute-done.2.m3, ...), custom_call_target="tpu_custom_call" | custom-call | flops 2000000000 | bytes 6000000 | tf_op jit(solution)/shard_map/traces/pallas_call | solution.py:309
  (19 shorter events, 0.1 us)
Async XLA Ops:
  5.8 8.2 %copy-start.8 = (bf16[2,4,4,128]{3,2,1,0:T(4,128)(2,1)S(1)}, bf16[2,4,4,128]{3,2,1,0:T(4,128)(2,1)}, u32[]{:S(2)}) copy-start(bf16[2,4,4,128]{3,2,1,0:T(4,128)(2,1)} %constant.32) | copy-start | bytes 24580
  5.8 8.8 %copy-start.2 = (bf16[2,2,256,128]{3,2,1,0:T(8,128)(2,1)S(1)}, bf16[2,2,256,128]{3,2,1,0:T(8,128)(2,1)}, u32[]{:S(2)}) copy-start(bf16[2,2,256,128]{3,2,1,0:T(8,128)(2,1)} %recorded_hbm.3) | copy-start | bytes 786436
  5.8 8.8 %copy-start.3 = (s32[2,32,32]{2,1,0:T(8,128)S(1)}, s32[2,32,32]{2,1,0:T(8,128)}, u32[]{:S(2)}) copy-start(s32[2,32,32]{2,1,0:T(8,128)} %param.10) | copy-start | bytes 24580
  5.9 36.9 %all-to-all-start = ((bf16[32,128,256]{2,1,0:T(8,128)(2,1)}), bf16[32,128,256]{2,1,0:T(8,128)(2,1)S(1)}, u32[]{:S(2)}, u32[]{:S(2)}) async-start(bf16[32,128,256]{2,1,0:T(8,128)(2,1)} %blocks.1), calls=%async_computation | async-start | bytes 4194304 | tf_op jit(solution)/shard_map/all_to_all | solution.py:357
  14.7 3.4 %copy-start = (bf16[2,32,2,256,128]{4,3,2,1,0:T(8,128)(2,1)S(1)}, bf16[2,32,2,256,128]{4,3,2,1,0:T(8,128)(2,1)}, u32[]{:S(2)}) copy-start(bf16[2,32,2,256,128]{4,3,2,1,0:T(8,128)(2,1)} %v_hbm.3) | copy-start | bytes 25165828
  18.1 3.4 %copy-start.1 = (bf16[2,2,256,32,128]{4,3,2,1,0:T(8,128)(2,1)S(1)}, bf16[2,2,256,32,128]{4,3,2,1,0:T(8,128)(2,1)}, u32[]{:S(2)}) copy-start(bf16[2,2,256,32,128]{4,3,2,1,0:T(8,128)(2,1)} %u_hbm.1) | copy-start | bytes 25165828
  21.4 30.9 %copy-start.7 = (s32[256,32]{0,1:T(8,128)S(1)}, s32[256,32]{0,1:T(8,128)}, u32[]{:S(2)}) copy-start(s32[256,32]{0,1:T(8,128)} %param.11) | copy-start | bytes 98308
  21.4 36.3 %copy-start.6 = (bf16[128,1024]{1,0:T(8,128)(2,1)S(1)}, bf16[128,1024]{1,0:T(8,128)(2,1)}, u32[]{:S(2)}) copy-start(bf16[128,1024]{1,0:T(8,128)(2,1)} %constant.27.clone.spread_ref) | copy-start | bytes 786436
  35.7 2.0 %copy-start.4 = (bf16[2,512,2048]{2,1,0:T(8,128)(2,1)}, bf16[2,512,2048]{2,1,0:T(8,128)(2,1)S(1)}, u32[]{:S(2)}) copy-start(bf16[2,512,2048]{2,1,0:T(8,128)(2,1)S(1)} %get-tuple-element.12.packed_ref) | copy-start | bytes 12582916
  42.8 2.2 %copy-start.5 = (bf16[2,512,2048]{2,1,0:T(8,128)(2,1)S(1)}, bf16[2,512,2048]{2,1,0:T(8,128)(2,1)}, u32[]{:S(2)}) copy-start(bf16[2,512,2048]{2,1,0:T(8,128)(2,1)} %copy-done.4) | copy-start | bytes 12582916
  46.6 5.9 %collective-permute-start = (bf16[4,64,128]{2,1,0:T(8,128)(2,1)S(1)}, bf16[4,64,128]{2,1,0:T(8,128)(2,1)S(1)}, u32[]{:S(2)}, u32[]{:S(2)}) collective-permute-start(bf16[4,64,128]{2,1,0:T(8,128)(2,1)S(1)} %get-tuple-element.16), channel_id=1, source_target_pairs={{0,32},{32,0},{64,96},{96,64},{1,33},{33,1},{65,97},{97,65},{2,34}... | collective-permute-start | bytes 196616 | tf_op jit(solution)/shard_map/ppermute | solution.py:365
  48.7 6.6 %collective-permute-start.1 = (bf16[4,64,128]{2,1,0:T(8,128)(2,1)S(1)}, bf16[4,64,128]{2,1,0:T(8,128)(2,1)S(1)}, u32[]{:S(2)}, u32[]{:S(2)}) collective-permute-start(bf16[4,64,128]{2,1,0:T(8,128)(2,1)S(1)} %get-tuple-element.17), channel_id=1, source_target_pairs={{0,64},{32,96},{64,0},{96,32},{1,65},{33,97},{65,1},{97,33},{2,66}... | collective-permute-start | bytes 196616 | tf_op jit(solution)/shard_map/ppermute | solution.py:365
  52.3 5.5 %collective-permute-start.2 = (bf16[4,64,128]{2,1,0:T(8,128)(2,1)S(1)}, bf16[4,64,128]{2,1,0:T(8,128)(2,1)S(1)}, u32[]{:S(2)}, u32[]{:S(2)}) collective-permute-start(bf16[4,64,128]{2,1,0:T(8,128)(2,1)S(1)} %get-tuple-element.18), channel_id=1, source_target_pairs={{0,96},{32,64},{64,32},{96,0},{1,97},{33,65},{65,33},{97,1},{2,98}... | collective-permute-start | bytes 196616 | tf_op jit(solution)/shard_map/ppermute | solution.py:365

commit v3 on v2

--- a/solution.py
+++ b/solution.py
@@ -46,13 +46,13 @@
 GROUP = 8
 
 
-def order_tiles(order, rank_of, count):
+def order_tiles(order, rank_of, first, end):
     def place(i, n):
         some = rank_of(i) > 0
-        order[jnp.where(some, n, count - 1 - (i - n))] = i
+        order[jnp.where(some, n, end - 1 - (i - n))] = i
         return n + some.astype(jnp.int32)
 
-    return lax.fori_loop(0, count, place, jnp.int32(0))
+    return lax.fori_loop(first, end, place, jnp.int32(0))
 
 
 def blocks_kernel(
@@ -63,8 +63,14 @@
     tile_count = factors.shape[1]
     get_ranks = pltpu.make_async_copy(ranks_hbm, ranks, small_sem.at[0])
     get_recorded = pltpu.make_async_copy(recorded_hbm, recorded, small_sem.at[1])
+    def get_first(f):
+        first = pl.ds(0, GROUP)
+        return pltpu.make_async_copy(v_hbm.at[f, first], factors.at[f, first], v_sem.at[f, 0])
+
     get_ranks.start()
     get_recorded.start()
+    for f in range(2):
+        get_first(f).start()
     empty[...] = jnp.zeros_like(empty)
 
     def get_tile(f, i):
@@ -92,17 +98,29 @@
 
             return rank
 
-        counts.append(order_tiles(order.at[f], rank_of, tile_count))
+        counts.append(order_tiles(order.at[f], rank_of, GROUP, tile_count))
     groups = [(n + GROUP - 1) // GROUP for n in counts]
     for f in range(2):
 
-        @pl.loop(groups[f] * GROUP, tile_count)
+        @pl.loop(groups[f] * GROUP, tile_count - GROUP)
         def _(n):
             put_empty(f, order[f, n]).start()
 
     get_recorded.wait()
     stack_sources(recorded, stacked)
     row = row_index((64, 256))
+
+    def multiply(f, tiles):
+        for i in tiles:
+            product = transposed_dot(factors[f, i], stacked[f])[0:64]
+            kept = row < ranks[tile_count * f + i, column]
+            blocks[f, i] = jnp.where(kept, product, 0.0).astype(jnp.bfloat16)
+        for i in tiles:
+            put_tile(f, i).start()
+
+    for f in range(2):
+        get_first(f).wait()
+        multiply(f, range(GROUP))
     for f in range(2):
 
         @pl.loop(0, groups[f])
@@ -114,12 +132,7 @@
                 def _():
                     get_tile(f, i).wait()
 
-            for i in tiles:
-                product = transposed_dot(factors[f, i], stacked[f])[0:64]
-                kept = row < ranks[tile_count * f + i, column]
-                blocks[f, i] = jnp.where(kept, product, 0.0).astype(jnp.bfloat16)
-            for i in tiles:
-                put_tile(f, i).start()
+            multiply(f, tiles)
 
     for f in range(2):
 
@@ -233,7 +246,7 @@
             pltpu.SemaphoreType.DMA((4,)),
             pltpu.SemaphoreType.DMA((2,)),
         ],
-        compiler_params=params(16),
+        compiler_params=params(50),
         cost_estimate=pl.CostEstimate(
             flops=2 * 10**8, bytes_accessed=40 * 10**6, transcendentals=0
         ),
@@ -293,7 +306,7 @@
             start_ref[r * 128 : (r + 1) * 128, :] = start.T.astype(jnp.bfloat16)
 
     traces = jnp.dot(left_ref[...], basis_ref[...], preferred_element_type=jnp.float32)
-    start = jnp.dot(start_ref[...], spread_ref[...], preferred_element_type=jnp.float32)
+    start = jnp.dot(start_ref[:, 0:16], spread_ref[...], preferred_element_type=jnp.float32)
     times = lane_index((8, 4, 32, 128)).astype(jnp.float32)
     for p in range(out_ref.shape[2]):
         lanes = slice(p * 128, (p + 1) * 128)
@@ -313,7 +326,7 @@
         + [
             pl.BlockSpec((64, 128), lambda s: (0, 0)),
             pl.BlockSpec((256, width * NT), lambda s: (0, s)),
-            pl.BlockSpec((128, width * NT), lambda s: (0, s)),
+            pl.BlockSpec((16, width * NT), lambda s: (0, s)),
         ],
         out_specs=pl.BlockSpec((4, 8, width, 32, NT), lambda s: (0, 0, s, 0, 0)),
         out_shape=jax.ShapeDtypeStruct((4, 8, 8, 32, 128), jnp.float32),
@@ -345,10 +358,10 @@
     rows = jnp.take(both, group ^ jnp.arange(4, dtype=jnp.int32), axis=1).reshape(2, 16, NT)
     same = jnp.eye(8, dtype=jnp.bfloat16)
     basis = (rows[:, :, None, None, :] * same[None, None, :, :, None]).reshape(256, 8 * NT)
-    spread = np.zeros((128, 8, NT), np.float32)
+    spread = np.zeros((16, 8, NT), np.float32)
     for p in range(8):
         spread[p, p] = 1.0
-    return basis, jnp.asarray(spread.reshape(128, 8 * NT), dtype=jnp.bfloat16)
+    return basis, jnp.asarray(spread.reshape(16, 8 * NT), dtype=jnp.bfloat16)
 
 
 def shards(recorded, v_factors, u_factors, tile_ranks, mute_start):

time: 61.1 us -> 61.1 us (level)
  local copies, waits for them, and re-layouts: 11.9 us -> 3.13 us
  waiting for transfers between devices: 10.2 us -> 17 us
  Pallas kernels: 24.7 us -> 27.3 us
    unnamed x18 -> x12, local copies, waits for them, and re-layouts: 11 us -> 2.22 us
    all_to_all x1, waiting for transfers between devices: 5.04 us -> 11.8 us  [shards(): lax.all_to_all(send, 'space', split_axis=0, concat_axis=0, tiled=True)]
    pallas_call x1, Pallas kernels: 14.2 us -> 16.2 us  [prepare(): pl.pallas_call(prepare_kernel, in_specs=[pl.BlockSpec(memory_space=pltpu....]
  transfers between devices with their start and end apart: 4 -> 4, of which waited for: 3 -> 3; matrix products, arithmetic and copies ran while one was open for 2% -> 2% of each run, Pallas kernels for 23% -> 27%
where the time goes in v3:
time: 61.1 us; the launch traced here: 60.9 us
  Pallas kernels  27.3 us (45%)
  waiting for transfers between devices  17 us (28%)
  starting transfers between devices  13.1 us (21%)
  local copies, waits for them, and re-layouts  3.13 us (5%)
    pallas_call x1, Pallas kernels, prepare(): pl.pallas_call(prepare_kernel, in_specs=[pl.BlockSpec(memory_space=pltpu....  16.2 us
    all_to_all x1, waiting for transfers between devices, shards(): lax.all_to_all(send, 'space', split_axis=0, concat_axis=0, tiled=True)  11.8 us
    all_to_all x1, starting transfers between devices, shards(): lax.all_to_all(send, 'space', split_axis=0, concat_axis=0, tiled=True)  7.54 us
    pallas_call x1, Pallas kernels, make_blocks(): pl.pallas_call(blocks_kernel, in_specs=[pl.BlockSpec(memory_space=pltpu.H...  6.42 us
    ppermute x3, starting transfers between devices, shards(): arrived.append(lax.ppermute(messages[m], 'freq', pairs))  5.59 us
    ppermute x3, waiting for transfers between devices, shards(): arrived.append(lax.ppermute(messages[m], 'freq', pairs))  5.17 us
    pallas_call x1, Pallas kernels, make_traces(): pl.pallas_call(traces_kernel, grid=(8 // width,), in_specs=[message] * 4...  3.02 us
    unnamed x12, local copies, waits for them, and re-layouts  2.22 us
  transfers between devices with their start and end apart: 4, of which 3 were waited for; matrix products, arithmetic and copies ran while one was open for 2% of the time, Pallas kernels for 27%

profile of v3, /device:TPU:0, one launch (start us, length us, event | category | flops | bytes accessed | tf_op | source)
XLA Modules:
  0.0 60.9 jit_solution(16351502737621465391)
XLA Ops:
  0.0 6.4 %blocks.1 = bf16[32,128,256]{2,1,0:T(8,128)(2,1)} custom-call(s32[64,32]{1,0:T(8,128)} %bitcast.13, bf16[2,2,256,128]{3,2,1,0:T(8,128)(2,1)} %recorded_hbm.3, bf16[2,32,2,256,128]{4,3,2,1,0:T(8,128)(2,1)} %v_hbm.3), custom_call_target="tpu_custom_call" | custom-call | flops 4000000000 | bytes 11000000 | tf_op jit(solution)/shard_map/blocks/pallas_call | solution.py:146
  6.4 0.0 copy-start.5
  6.4 0.0 copy-start
  6.5 0.0 copy-start.1
  6.5 7.5 %all-to-all-start = ((bf16[32,128,256]{2,1,0:T(8,128)(2,1)}), bf16[32,128,256]{2,1,0:T(8,128)(2,1)S(1)}, u32[]{:S(2)}, u32[]{:S(2)}) async-start(bf16[32,128,256]{2,1,0:T(8,128)(2,1)} %blocks.1), calls=%async_computation | async-start | bytes 4194304 | tf_op jit(solution)/shard_map/all_to_all | solution.py:370
  14.0 0.1 broadcast_in_dim.15
  14.1 0.1 broadcast_in_dim.16
  14.2 0.6 gather_fusion
  14.8 0.0 copy-start.4
  14.8 0.0 copy-start.3
  14.8 16.2 %prepare.1 = (bf16[2,512,2048]{2,1,0:T(8,128)(2,1)}, bf16[2,512,128]{2,1,0:T(8,128)(2,1)S(1)}, bf16[128,256]{1,0:T(8,128)(2,1)S(1)}) custom-call(s32[64,32]{1,0:T(8,128)S(1)} %bitcast.14, bf16[2,2,256,128]{3,2,1,0:T(8,128)(2,1)S(1)} %copy-done, bf16[2,32,2,256,128]{4,3,2,1,0:T(8,128)(2,1)} %v_hbm.3, bf16[2,2,256,32,128]{4,3,2,1,0:T(8,128)(2,1)} %u_hbm.1), custom_call_target="tpu_custom_call" | custom-call | flops 200000000 | bytes 40000000 | tf_op jit(solution)/shard_map/prepare/pallas_call | solution.py:230
  31.1 0.1 broadcast_select_fusion
  31.1 11.8 %all-to-all-done.received_ref = bf16[32,128,256]{2,1,0:T(8,128)(2,1)S(1)} async-done(((bf16[32,128,256]{2,1,0:T(8,128)(2,1)}), bf16[32,128,256]{2,1,0:T(8,128)(2,1)S(1)}, u32[]{:S(2)}, u32[]{:S(2)}) %all-to-all-start) | async-done | bytes 2097184 | tf_op jit(solution)/shard_map/all_to_all | solution.py:370
  42.9 2.2 %copy-done.2 = bf16[2,512,2048]{2,1,0:T(8,128)(2,1)S(1)} copy-done((bf16[2,512,2048]{2,1,0:T(8,128)(2,1)S(1)}, bf16[2,512,2048]{2,1,0:T(8,128)(2,1)}, u32[]{:S(2)}) %copy-start.2) | copy-done | bytes 4194328
  45.1 1.6 %spectra.1 = (bf16[4,64,128]{2,1,0:T(8,128)(2,1)S(1)}, bf16[4,64,128]{2,1,0:T(8,128)(2,1)S(1)}, bf16[4,64,128]{2,1,0:T(8,128)(2,1)S(1)}, bf16[4,64,128]{2,1,0:T(8,128)(2,1)S(1)}) custom-call(bf16[2,512,2048]{2,1,0:T(8,128)(2,1)S(1)} %copy-done.2, bf16[2,512,128]{2,1,0:T(8,128)(2,1)S(1)} %get-tuple-element.13.own_ref, ...), custom_call_target="tpu_custom_call" | custom-call | flops 2000000000 | bytes 7000000 | tf_op jit(solution)/shard_map/spectra/pallas_call | solution.py:281
  46.8 2.0 %collective-permute-start = (bf16[4,64,128]{2,1,0:T(8,128)(2,1)S(1)}, bf16[4,64,128]{2,1,0:T(8,128)(2,1)S(1)}, u32[]{:S(2)}, u32[]{:S(2)}) collective-permute-start(bf16[4,64,128]{2,1,0:T(8,128)(2,1)S(1)} %get-tuple-element.16), channel_id=1, source_target_pairs={{0,32},{32,0},{64,96},{96,64},{1,33},{33,1},{65,97},{97,65},{2,34}... | collective-permute-start | bytes 196616 | tf_op jit(solution)/shard_map/ppermute | solution.py:378
  48.8 3.6 %collective-permute-start.1 = (bf16[4,64,128]{2,1,0:T(8,128)(2,1)S(1)}, bf16[4,64,128]{2,1,0:T(8,128)(2,1)S(1)}, u32[]{:S(2)}, u32[]{:S(2)}) collective-permute-start(bf16[4,64,128]{2,1,0:T(8,128)(2,1)S(1)} %get-tuple-element.17), channel_id=1, source_target_pairs={{0,64},{32,96},{64,0},{96,32},{1,65},{33,97},{65,1},{97,33},{2,66}... | collective-permute-start | bytes 196616 | tf_op jit(solution)/shard_map/ppermute | solution.py:378
  52.4 0.1 broadcast_multiply_fusion
  52.5 0.1 reshape.55
  52.6 0.1 copy.13.mute_ref
  52.7 0.0 collective-permute-done.m1
  52.7 2.7 %collective-permute-done.1.m2 = bf16[4,64,128]{2,1,0:T(8,128)(2,1)S(1)} collective-permute-done((bf16[4,64,128]{2,1,0:T(8,128)(2,1)S(1)}, bf16[4,64,128]{2,1,0:T(8,128)(2,1)S(1)}, u32[]{:S(2)}, u32[]{:S(2)}) %collective-permute-start.1) | collective-permute-done | bytes 65568 | tf_op jit(solution)/shard_map/ppermute | solution.py:378
  55.4 2.4 %collective-permute-done.2.m3 = bf16[4,64,128]{2,1,0:T(8,128)(2,1)S(1)} collective-permute-done((bf16[4,64,128]{2,1,0:T(8,128)(2,1)S(1)}, bf16[4,64,128]{2,1,0:T(8,128)(2,1)S(1)}, u32[]{:S(2)}, u32[]{:S(2)}) %collective-permute-start.2) | collective-permute-done | bytes 65568 | tf_op jit(solution)/shard_map/ppermute | solution.py:378
  57.8 3.0 %traces.1 = f32[4,8,8,32,128]{4,3,2,1,0:T(8,128)} custom-call(bf16[4,64,128]{2,1,0:T(8,128)(2,1)S(1)} %get-tuple-element.15.m0, bf16[4,64,128]{2,1,0:T(8,128)(2,1)S(1)} %collective-permute-done.m1, bf16[4,64,128]{2,1,0:T(8,128)(2,1)S(1)} %collective-permute-done.1.m2, bf16[4,64,128]{2,1,0:T(8,128)(2,1)S(1)} %collective-permute-done.2.m3, ...), custom_call_target="tpu_custom_call" | custom-call | flops 2000000000 | bytes 6000000 | tf_op jit(solution)/shard_map/traces/pallas_call | solution.py:322
  (13 shorter events, 0.1 us)
Async XLA Ops:
  6.4 7.8 %copy-start.5 = (bf16[2,4,4,128]{3,2,1,0:T(4,128)(2,1)S(1)}, bf16[2,4,4,128]{3,2,1,0:T(4,128)(2,1)}, u32[]{:S(2)}) copy-start(bf16[2,4,4,128]{3,2,1,0:T(4,128)(2,1)} %constant.32) | copy-start | bytes 24580
  6.4 8.4 %copy-start = (bf16[2,2,256,128]{3,2,1,0:T(8,128)(2,1)S(1)}, bf16[2,2,256,128]{3,2,1,0:T(8,128)(2,1)}, u32[]{:S(2)}) copy-start(bf16[2,2,256,128]{3,2,1,0:T(8,128)(2,1)} %recorded_hbm.3) | copy-start | bytes 786436
  6.5 8.4 %copy-start.1 = (s32[2,32,32]{2,1,0:T(8,128)S(1)}, s32[2,32,32]{2,1,0:T(8,128)}, u32[]{:S(2)}) copy-start(s32[2,32,32]{2,1,0:T(8,128)} %param.10) | copy-start | bytes 24580
  6.5 36.5 %all-to-all-start = ((bf16[32,128,256]{2,1,0:T(8,128)(2,1)}), bf16[32,128,256]{2,1,0:T(8,128)(2,1)S(1)}, u32[]{:S(2)}, u32[]{:S(2)}) async-start(bf16[32,128,256]{2,1,0:T(8,128)(2,1)} %blocks.1), calls=%async_computation | async-start | bytes 4194304 | tf_op jit(solution)/shard_map/all_to_all | solution.py:370
  14.8 37.7 %copy-start.4 = (s32[256,32]{0,1:T(8,128)S(1)}, s32[256,32]{0,1:T(8,128)}, u32[]{:S(2)}) copy-start(s32[256,32]{0,1:T(8,128)} %param.11) | copy-start | bytes 98308
  14.8 43.0 %copy-start.3 = (bf16[16,1024]{1,0:T(8,128)(2,1)S(1)}, bf16[16,1024]{1,0:T(8,128)(2,1)}, u32[]{:S(2)}) copy-start(bf16[16,1024]{1,0:T(8,128)(2,1)} %constant.27.clone.spread_ref) | copy-start | bytes 98308
  42.9 2.2 %copy-start.2 = (bf16[2,512,2048]{2,1,0:T(8,128)(2,1)S(1)}, bf16[2,512,2048]{2,1,0:T(8,128)(2,1)}, u32[]{:S(2)}) copy-start(bf16[2,512,2048]{2,1,0:T(8,128)(2,1)} %get-tuple-element.12.packed_ref) | copy-start | bytes 12582916
  46.8 5.9 %collective-permute-start = (bf16[4,64,128]{2,1,0:T(8,128)(2,1)S(1)}, bf16[4,64,128]{2,1,0:T(8,128)(2,1)S(1)}, u32[]{:S(2)}, u32[]{:S(2)}) collective-permute-start(bf16[4,64,128]{2,1,0:T(8,128)(2,1)S(1)} %get-tuple-element.16), channel_id=1, source_target_pairs={{0,32},{32,0},{64,96},{96,64},{1,33},{33,1},{65,97},{97,65},{2,34}... | collective-permute-start | bytes 196616 | tf_op jit(solution)/shard_map/ppermute | solution.py:378
  48.8 6.6 %collective-permute-start.1 = (bf16[4,64,128]{2,1,0:T(8,128)(2,1)S(1)}, bf16[4,64,128]{2,1,0:T(8,128)(2,1)S(1)}, u32[]{:S(2)}, u32[]{:S(2)}) collective-permute-start(bf16[4,64,128]{2,1,0:T(8,128)(2,1)S(1)} %get-tuple-element.17), channel_id=1, source_target_pairs={{0,64},{32,96},{64,0},{96,32},{1,65},{33,97},{65,1},{97,33},{2,66}... | collective-permute-start | bytes 196616 | tf_op jit(solution)/shard_map/ppermute | solution.py:378
  52.4 5.5 %collective-permute-start.2 = (bf16[4,64,128]{2,1,0:T(8,128)(2,1)S(1)}, bf16[4,64,128]{2,1,0:T(8,128)(2,1)S(1)}, u32[]{:S(2)}, u32[]{:S(2)}) collective-permute-start(bf16[4,64,128]{2,1,0:T(8,128)(2,1)S(1)} %get-tuple-element.18), channel_id=1, source_target_pairs={{0,96},{32,64},{64,32},{96,0},{1,97},{33,65},{65,33},{97,1},{2,98}... | collective-permute-start | bytes 196616 | tf_op jit(solution)/shard_map/ppermute | solution.py:378
